TPU v7x, 256 devices: a whole 4x4x8 slice. The times are simulated.
256 devices in a mesh: dp: 32 (over y, x, core), seq: 8 (over z).
Axes of the slice: x: 4, y: 4, z: 8, core: 2. Of those that a mesh axis runs over, the one named last changes fastest.
Arguments:
- clip_table: int32 [64, 5], replicated, may hold values from 0 to 31, as said below
- attention_inputs: bfloat16 [3, 32768, 3072], P(None, ('dp', 'seq')), may hold values from -24 to 24
- out_weight: bfloat16 [3072, 5120], P(None, 'seq'), may hold values from -0.109375 to 0.109375
- adapter_down: bfloat16 [3072, 32], replicated, may hold values from -0.109375 to 0.109375
- adapter_up_weight: bfloat16 [32, 5120], replicated, may hold values from -1 to 1
- cotangent: bfloat16 [32768, 5120], P(('dp', 'seq')), may hold values from -0.078125 to 0.078125
Outputs:
- mixed: bfloat16 [32768, 5120], P(('dp', 'seq'))
- grad_down: float32 [3072, 32], replicated
- up_weight_gradient: float32 [32, 5120], replicated
Inputs may be any that keep to these rules, and one draw needn't show every extreme that they name: `clip_table`: each group is the destination of exactly 2 clips and the source of exactly 2 clips: one has it as both, each other one comes from a different group whose index differs from it in exactly one bit; the bits in which moved clips' groups differ are the same for all groups. Frames run from 1 to 8, heights from 2 to 4, widths are 8 or 16; every group receives one clip of exactly 512 tokens.
All inputs are finite; a program needn't handle non-finite values.
Results may differ from a plain program's by a relative error of at most 0.0094.
Values may be sent and summed in bfloat16 or wider, within the bound.
No kernel may reach another device: no remote copies, remote signals or barrier semaphores. Data moves between devices by JAX's collectives and lax.ppermute only.
A program may use at most 128 MiB of HBM per device.

v0:
```python
import math

import jax
import jax.numpy as jnp
from jax import lax
from jax.sharding import PartitionSpec as P

HEAD = 128
MAXP = 64


ADAPTER_SCALE = 2.0


def from_partner(block, axis, apart):
    count = lax.axis_size(axis)
    route = []
    for low in range(count):
        high = low | 1 << apart
        if high != low and high < count:
            route += [(low, high), (high, low)]
    return lax.ppermute(block, axis, route)


def rope_tables(frame_pos, height_pos, width_pos, head_size):
    sixth_share = head_size // 6
    axis_widths = (head_size - 4 * sixth_share, 2 * sixth_share, 2 * sixth_share)
    angle_parts = []
    for position, axis_width in zip((frame_pos, height_pos, width_pos), axis_widths):
        exponent = jnp.arange(0, axis_width, 2).astype(jnp.float32) / axis_width
        frequency = jnp.power(jnp.float32(10000.0), -exponent)
        angle_parts.append(position.astype(jnp.float32)[:, None] * frequency[None, :])
    angles = jnp.concatenate(angle_parts, axis=1)
    return (jnp.repeat(jnp.cos(angles), 2, axis=1), jnp.repeat(jnp.sin(angles), 2, axis=1))


def clip_layout(clip_table, shard_count):
    source = clip_table[:, 0]
    target = clip_table[:, 1]
    frames = clip_table[:, 2]
    height = clip_table[:, 3]
    widths = clip_table[:, 4]
    portion = frames * height * widths // shard_count
    ordinal = jnp.arange(clip_table.shape[0], dtype=jnp.int32)
    earlier = ordinal[None, :] < ordinal[:, None]
    source_offset = jnp.sum(
        jnp.where(earlier & (source[None, :] == source[:, None]), portion[None, :], 0), axis=1
    )
    target_offset = jnp.sum(
        jnp.where(earlier & (target[None, :] == target[:, None]), portion[None, :], 0), axis=1
    )
    return (source, target, height, widths, portion, source_offset, target_offset)


def rotate_rows(values, cosine_table, sine_table, swap_table, head_size):
    row_count = values.shape[0]
    heads_here = values.shape[1] // head_size
    swapped = jnp.dot(
        values.reshape(row_count * heads_here, head_size),
        swap_table,
        preferred_element_type=jnp.float32,
    )
    swapped = swapped.reshape(row_count, heads_here, head_size)
    widened = values.astype(jnp.float32).reshape(row_count, heads_here, head_size)
    turned = widened * cosine_table[:, None, :] + swapped * sine_table[:, None, :]
    return turned.reshape(row_count, heads_here * head_size).astype(jnp.bfloat16)


def body(clip_table, attention_inputs, out_weight, adapter_down, adapter_up_weight, cotangent):
    seq_count = lax.axis_size("seq")
    group_index = lax.axis_index("dp")
    seq_index = lax.axis_index("seq")
    rows_dev = cotangent.shape[0]
    slot_rows = MAXP
    head_size = HEAD
    source_rows = attention_inputs.shape[1]
    feature_dev = out_weight.shape[1]
    source, target, height, widths, portion, source_offset, target_offset = clip_layout(
        clip_table, seq_count
    )
    ordinal = jnp.arange(clip_table.shape[0], dtype=jnp.int32)
    row_index = jnp.arange(rows_dev, dtype=jnp.int32)
    slot_range = jnp.arange(slot_rows, dtype=jnp.int32)
    member = (
        (target[None, :] == group_index)
        & (row_index[:, None] >= target_offset[None, :])
        & (row_index[:, None] < (target_offset + portion)[None, :])
    )
    relative = row_index[:, None] - target_offset[None, :]

    def clip_value(values):
        return jnp.sum(jnp.where(member, values, 0), axis=1)

    valid_row = jnp.any(member, axis=1)
    clip_index = clip_value(ordinal[None, :] + 1) - 1
    row_height = jnp.where(valid_row, clip_value(height[None, :]), 1)
    row_width = jnp.where(valid_row, clip_value(widths[None, :]), 1)
    token_index = clip_value(seq_index * portion[None, :] + relative)
    frame_pos = token_index // (row_height * row_width)
    height_pos = token_index // row_width % row_height
    width_pos = token_index % row_width
    bit_count = lax.axis_size("dp").bit_length() - 1
    levels = jnp.arange(bit_count, dtype=jnp.int32)
    powers = jnp.left_shift(jnp.int32(1), levels)
    staying = (source == group_index) & (target == group_index)
    stay_start = jnp.sum(jnp.where(staying, source_offset, 0))
    stay_piece = jnp.take(
        attention_inputs, jnp.minimum(stay_start + slot_range, source_rows - 1), axis=1
    )
    difference = jnp.bitwise_xor(source, group_index)
    pieces = [stay_piece]
    for bit_level in range(bit_count):
        partner = jnp.bitwise_xor(group_index, 1 << bit_level)
        going = (source == group_index) & (target == partner)
        start_row = jnp.sum(jnp.where(going, source_offset, 0))
        outgoing = jnp.take(
            attention_inputs, jnp.minimum(start_row + slot_range, source_rows - 1), axis=1
        )
        pieces.append(from_partner(outgoing, "dp", bit_level))
    arrived = jnp.concatenate(pieces, axis=1)
    bit_of_clip = jnp.sum(
        jnp.where(difference[:, None] == powers[None, :], levels[None, :], 0), axis=1
    )
    slot_index = jnp.where(difference == 0, 0, 1 + bit_of_clip)
    gather_row = clip_value(slot_index[None, :] * slot_rows + relative)
    placed = jnp.take(arrived, gather_row, axis=1)
    placed = jnp.where(valid_row[None, :, None], placed, jnp.zeros((), jnp.bfloat16))
    cosine_table, sine_table = rope_tables(frame_pos, height_pos, width_pos, head_size)
    row_ids = jnp.arange(head_size, dtype=jnp.int32)[:, None]
    col_ids = jnp.arange(head_size, dtype=jnp.int32)[None, :]
    swap_table = jnp.where(
        (row_ids == col_ids + 1) & (col_ids % 2 == 0),
        -1.0,
        jnp.where((col_ids == row_ids + 1) & (row_ids % 2 == 0), 1.0, 0.0),
    ).astype(jnp.bfloat16)
    sectioned = jnp.stack(
        [
            rotate_rows(placed[0], cosine_table, sine_table, swap_table, head_size),
            rotate_rows(placed[1], cosine_table, sine_table, swap_table, head_size),
            placed[2],
        ],
        axis=0,
    )
    heads_view = lax.all_to_all(sectioned, "seq", split_axis=2, concat_axis=1, tiled=True)
    group_rows = heads_view.shape[1]
    heads_dev = heads_view.shape[2] // head_size
    queries = heads_view[0].reshape(group_rows, heads_dev, head_size)
    rotated_keys = heads_view[1].reshape(group_rows, heads_dev, head_size)
    head_values = heads_view[2].reshape(group_rows, heads_dev, head_size)
    clip_all = jnp.tile(clip_index, seq_count)
    valid_all = jnp.tile(valid_row, seq_count)
    same_clip = (clip_all[:, None] == clip_all[None, :]) & valid_all[:, None]
    att_scale = 1.0 / math.sqrt(head_size)
    head_results = []
    for head_number in range(heads_dev):
        scores = (
            jnp.dot(
                queries[:, head_number],
                rotated_keys[:, head_number].T,
                preferred_element_type=jnp.float32,
            )
            * att_scale
        )
        masked = jnp.where(same_clip, scores, -1e30)
        largest = jnp.max(masked, axis=1, keepdims=True)
        exponentials = jnp.where(same_clip, jnp.exp(masked - largest), 0.0)
        totals = jnp.sum(exponentials, axis=1, keepdims=True)
        totals = jnp.where(valid_all[:, None], totals, 1.0)
        probabilities = (exponentials / totals).astype(jnp.bfloat16)
        head_results.append(
            jnp.dot(probabilities, head_values[:, head_number], preferred_element_type=jnp.float32)
        )
    attended = jnp.stack(head_results, axis=1)
    attended = attended.reshape(group_rows, heads_dev * head_size).astype(jnp.bfloat16)
    hidden_gradient = (
        ADAPTER_SCALE * jnp.dot(cotangent, adapter_up_weight.T, preferred_element_type=jnp.float32)
    ).astype(jnp.bfloat16)
    incoming = lax.all_gather(attended, "seq", axis=1, tiled=True)
    own_rows = lax.dynamic_slice_in_dim(incoming, seq_index * rows_dev, rows_dev, 0)
    projected_output = jnp.dot(incoming, out_weight, preferred_element_type=jnp.float32)
    adapter_output = jnp.dot(incoming, adapter_down, preferred_element_type=jnp.float32)
    update = jnp.einsum("tk,tr->kr", own_rows, hidden_gradient, preferred_element_type=jnp.float32)
    grad_down = update
    projected_output, adapter_output, grad_down = (projected_output, adapter_output, grad_down)
    adapter_hidden = adapter_output.astype(jnp.bfloat16)
    up_weight_columns = lax.dynamic_slice_in_dim(
        adapter_up_weight, seq_index * feature_dev, feature_dev, 1
    )
    mixed_cols = (
        projected_output
        + ADAPTER_SCALE
        * jnp.dot(adapter_hidden, up_weight_columns, preferred_element_type=jnp.float32)
    ).astype(jnp.bfloat16)
    mixed = lax.all_to_all(mixed_cols, "seq", split_axis=0, concat_axis=1, tiled=True)
    own_adapted = lax.dynamic_slice_in_dim(adapter_hidden, seq_index * rows_dev, rows_dev, 0)
    up_weight_gradient = ADAPTER_SCALE * jnp.einsum(
        "tr,td->rd", own_adapted, cotangent, preferred_element_type=jnp.float32
    )
    grad_down, up_weight_gradient = lax.psum((grad_down, up_weight_gradient), ("dp", "seq"))
    return (mixed, grad_down, up_weight_gradient)


def solution(mesh):
    in_specs = (P(), P(None, ("dp", "seq"), None), P(None, "seq"), P(), P(), P(("dp", "seq"), None))
    out_specs = (P(("dp", "seq"), None), P(), P())
    return jax.shard_map(body, mesh=mesh, in_specs=in_specs, out_specs=out_specs, check_vma=False)
```

profile of v0, /device:TPU:1, one launch (start us, length us, event | category | flops | bytes accessed | tf_op | source)
XLA Modules:
  0.0 651.3 jit_solution(1133954666217279884)
XLA Ops:
  13.7 4.0 gather_fusion.2
  24.5 4.0 gather_fusion.3
  32.4 4.0 gather_fusion.4
  42.0 4.0 gather_fusion.5
  51.3 4.0 gather_fusion.6
  64.0 4.0 gather_fusion.1
  74.1 10.1 %collective-permute-done.2 = bf16[3,64,3072]{2,1,0:T(8,128)(2,1)} collective-permute-done((bf16[3,64,3072]{2,1,0:T(8,128)(2,1)}, bf16[3,64,3072]{2,1,0:T(8,128)(2,1)}, u32[]{:S(2)}, u32[]{:S(2)}) %collective-permute-start.2) | collective-permute-done | bytes 1179680 | tf_op jit(solution)/shard_map/ppermute | solution.py:22
  86.9 16.3 %collective-permute-done.4 = bf16[3,64,3072]{2,1,0:T(8,128)(2,1)} collective-permute-done((bf16[3,64,3072]{2,1,0:T(8,128)(2,1)}, bf16[3,64,3072]{2,1,0:T(8,128)(2,1)}, u32[]{:S(2)}, u32[]{:S(2)}) %collective-permute-start.4) | collective-permute-done | bytes 1179680 | tf_op jit(solution)/shard_map/ppermute | solution.py:22
  104.6 29.8 %copy.95 = bf16[3,384,3072]{2,0,1:T(4,128)(2,1)} copy(bf16[3,384,3072]{2,1,0:T(8,128)(2,1)S(1)} %constant_dynamic-update-slice_fusion) | data formatting | bytes 14155776 | tf_op jit(solution)/shard_map/concatenate | solution.py:120
  134.4 8.4 %gather_fusion = bf16[128,3,3072]{2,1,0:T(4,128)(2,1)} fusion(bf16[3,384,3072]{2,0,1:T(4,128)(2,1)} %copy.95, s32[1024]{0:T(1024)S(1)} %get-tuple-element.54), kind=kCustom, calls=%fused_computation.6 | custom fusion | bytes 4719104 | tf_op jit(solution)/shard_map/jit(_take)/gather | solution.py:126
  142.8 4.0 select_bitcast_fusion
  146.8 4.4 fusion.72
  164.1 7.8 %pad_maximum_fusion = bf16[3,128,3072]{2,0,1:T(4,128)(2,1)} fusion(bf16[1,128,3072]{2,0,1:T(2,128)(2,1)S(1)} %copy-done.5, bf16[1,128,3072]{2,0,1:T(2,128)(2,1)} %copy.101, bf16[1,128,3072]{2,0,1:T(2,128)(2,1)} %copy.100), kind=kLoop, calls=%fused_computation.21 | loop fusion | flops 7077888 | bytes 4718592 | tf_op jit(solution)/shard_map/stack | solution.py:136
  172.0 7.5 %copy.102 = bf16[3,128,3072]{1,0,2:T(4,128)(2,1)} copy(bf16[3,128,3072]{2,0,1:T(4,128)(2,1)} %pad_maximum_fusion) | data formatting | bytes 4718592 | tf_op jit(solution)/shard_map/stack | solution.py:136
  179.4 8.2 %all-to-all-start = ((bf16[3,128,3072]{1,0,2:T(4,128)(2,1)}), bf16[3,128,3072]{1,0,2:T(4,128)(2,1)}, u32[]{:S(2)}, u32[]{:S(2)}) async-start(bf16[3,128,3072]{1,0,2:T(4,128)(2,1)} %copy.102), calls=%async_computation | async-start | bytes 6291456 | tf_op jit(solution)/shard_map/all_to_all | solution.py:144
  187.7 74.3 %all-to-all-done = bf16[3,128,3072]{1,0,2:T(4,128)(2,1)} async-done(((bf16[3,128,3072]{1,0,2:T(4,128)(2,1)}), bf16[3,128,3072]{1,0,2:T(4,128)(2,1)}, u32[]{:S(2)}, u32[]{:S(2)}) %all-to-all-start) | async-done | bytes 2359328 | tf_op jit(solution)/shard_map/all_to_all | solution.py:144
  273.5 4.9 fusion
  279.5 4.1 fusion.14
  290.3 66.1 %all-gather.2.cloned.1.call-done = bf16[1024,3072]{0,1:T(8,128)(2,1)} async-done(((bf16[1024,384]{0,1:T(8,128)(2,1)}), bf16[1024,3072]{0,1:T(8,128)(2,1)}) %all-gather.2.cloned.1.call-update) | async-done | bytes 6291472 | tf_op jit(solution)/shard_map/all_gather | solution.py:178
  356.4 4.1 convolution_convert_fusion
  361.0 7.6 %fusion.74 = f32[1024,640]{1,0:T(8,128)S(1)} fusion(bf16[1024,3072]{0,1:T(8,128)(2,1)S(1)} %copy-done.4, bf16[3072,640]{1,0:T(8,128)(2,1)} %param.10), kind=kOutput, calls=%fused_computation.199 | convolution fusion | flops 4026531840 | bytes 12845056 | tf_op jit(solution)/shard_map/dot_general | solution.py:180
  370.2 4.3 all-to-all-start.1
  379.4 29.5 %all-to-all-done.1 = bf16[8,128,640]{2,1,0:T(8,128)(2,1)} async-done(((bf16[8,128,640]{2,1,0:T(8,128)(2,1)}), bf16[8,128,640]{2,1,0:T(8,128)(2,1)}, u32[]{:S(2)}, u32[]{:S(2)}) %all-to-all-start.1) | async-done | bytes 1310752 | tf_op jit(solution)/shard_map/all_to_all | solution.py:194
  411.4 228.9 %all-reduce.3.cloned.1.call-done = (f32[3072,32]{0,1:T(8,128)}, f32[32,5120]{1,0:T(8,128)}) async-done(((f32[3072,32]{0,1:T(8,128)}, f32[32,5120]{1,0:T(8,128)}), (f32[3072,32]{0,1:T(8,128)}, f32[32,5120]{1,0:T(8,128)})) %all-reduce.3.cloned.1.call-update) | async-done | bytes 1048592 | tf_op jit(solution)/shard_map/psum | solution.py:199
  (115 shorter events, 92.1 us)
Async XLA Ops:
  7.2 6.5 copy-start
  19.5 51.9 %collective-permute-start = (bf16[3,64,3072]{2,1,0:T(8,128)(2,1)}, bf16[3,64,3072]{2,1,0:T(8,128)(2,1)}, u32[]{:S(2)}, u32[]{:S(2)}) collective-permute-start(bf16[3,64,3072]{2,1,0:T(8,128)(2,1)} %select_bitcast_fusion.5), channel_id=1, source_target_pairs={{0,8},{8,0},{16,24},{24,16},{32,40},{40,32},{48,56},{56,48},{64,72... | collective-permute-start | bytes 3538952 | tf_op jit(solution)/shard_map/ppermute | solution.py:22
  30.4 42.4 %collective-permute-start.1 = (bf16[3,64,3072]{2,1,0:T(8,128)(2,1)}, bf16[3,64,3072]{2,1,0:T(8,128)(2,1)}, u32[]{:S(2)}, u32[]{:S(2)}) collective-permute-start(bf16[3,64,3072]{2,1,0:T(8,128)(2,1)} %select_bitcast_fusion.4), channel_id=1, source_target_pairs={{0,16},{16,0},{8,24},{24,8},{32,48},{48,32},{40,56},{56,40},{64,80... | collective-permute-start | bytes 3538952 | tf_op jit(solution)/shard_map/ppermute | solution.py:22
  38.2 46.0 %collective-permute-start.2 = (bf16[3,64,3072]{2,1,0:T(8,128)(2,1)}, bf16[3,64,3072]{2,1,0:T(8,128)(2,1)}, u32[]{:S(2)}, u32[]{:S(2)}) collective-permute-start(bf16[3,64,3072]{2,1,0:T(8,128)(2,1)} %select_bitcast_fusion.3), channel_id=1, source_target_pairs={{0,32},{32,0},{8,40},{40,8},{16,48},{48,16},{24,56},{56,24},{64,96... | collective-permute-start | bytes 3538952 | tf_op jit(solution)/shard_map/ppermute | solution.py:22
  47.9 37.7 %collective-permute-start.3 = (bf16[3,64,3072]{2,1,0:T(8,128)(2,1)}, bf16[3,64,3072]{2,1,0:T(8,128)(2,1)}, u32[]{:S(2)}, u32[]{:S(2)}) collective-permute-start(bf16[3,64,3072]{2,1,0:T(8,128)(2,1)} %select_bitcast_fusion.2), channel_id=1, source_target_pairs={{0,64},{64,0},{8,72},{72,8},{16,80},{80,16},{24,88},{88,24},{32,96... | collective-permute-start | bytes 3538952 | tf_op jit(solution)/shard_map/ppermute | solution.py:22
  57.2 46.0 %collective-permute-start.4 = (bf16[3,64,3072]{2,1,0:T(8,128)(2,1)}, bf16[3,64,3072]{2,1,0:T(8,128)(2,1)}, u32[]{:S(2)}, u32[]{:S(2)}) collective-permute-start(bf16[3,64,3072]{2,1,0:T(8,128)(2,1)} %select_bitcast_fusion.1), channel_id=1, source_target_pairs={{0,128},{128,0},{8,136},{136,8},{16,144},{144,16},{24,152},{152,24... | collective-permute-start | bytes 3538952 | tf_op jit(solution)/shard_map/ppermute | solution.py:22
  63.5 0.5 copy-start.11
  160.4 3.7 copy-start.5
  179.4 82.5 %all-to-all-start = ((bf16[3,128,3072]{1,0,2:T(4,128)(2,1)}), bf16[3,128,3072]{1,0,2:T(4,128)(2,1)}, u32[]{:S(2)}, u32[]{:S(2)}) async-start(bf16[3,128,3072]{1,0,2:T(4,128)(2,1)} %copy.102), calls=%async_computation | async-start | bytes 6291456 | tf_op jit(solution)/shard_map/all_to_all | solution.py:144
  187.6 168.8 %all-gather.2.cloned.1.call-start = ((), (), s32[]{:S(2)}) async-start(), calls=%async_computation.2 | async-start | bytes 7077888 | tf_op jit(solution)/shard_map/all_gather | solution.py:178
  265.2 1.1 copy-start.7
  267.2 5.4 copy-start.8
  273.5 4.9 copy-start.2
  273.5 6.0 copy-start.3
  287.4 69.0 %copy-start.10 = (bf16[3072,32]{0,1:T(8,128)(2,1)S(1)}, bf16[3072,32]{0,1:T(8,128)(2,1)}, u32[]{:S(2)}) copy-start(bf16[3072,32]{0,1:T(8,128)(2,1)} %param.11) | copy-start | bytes 589828
  356.4 4.6 copy-start.4
  361.0 7.6 %copy-start.9 = (bf16[32,5120]{1,0:T(8,128)(2,1)S(1)}, bf16[32,5120]{1,0:T(8,128)(2,1)}, u32[]{:S(2)}) copy-start(bf16[32,5120]{1,0:T(8,128)(2,1)} %param.12) | copy-start | bytes 983044
  368.6 5.9 copy-start.6
  370.2 38.6 %all-to-all-start.1 = ((bf16[8,128,640]{2,1,0:T(8,128)(2,1)}), bf16[8,128,640]{2,1,0:T(8,128)(2,1)}, u32[]{:S(2)}, u32[]{:S(2)}) async-start(bf16[8,128,640]{2,1,0:T(8,128)(2,1)} %bitcast.152), calls=%async_computation.1 | async-start | bytes 2621440 | tf_op jit(solution)/shard_map/all_to_all | solution.py:194
  374.5 265.8 %all-reduce.3.cloned.1.call-start = ((), (), s32[]{:S(2)}) async-start(), calls=%async_computation.3 | async-start | bytes 2097152 | tf_op jit(solution)/shard_map/psum | solution.py:199
  375.7 268.3 %copy-start.1 = (bf16[3,128,3072]{2,1,0:T(8,128)(2,1)S(1)}, bf16[3,128,3072]{2,1,0:T(8,128)(2,1)}, u32[]{:S(2)}) copy-start(bf16[3,128,3072]{2,1,0:T(8,128)(2,1)} %param.9) | copy-start | bytes 7077892
Sparse Core Ops, SparseCore 0:
  290.4 65.9 all-gather.1
  381.6 258.7 all-reduce.2
where the time goes:
time: 660 us; the launch traced here: 651 us
  waiting for transfers between devices  425 us (64%)
  local copies, waits for them, and re-layouts  107 us (16%)
  other arithmetic  46.9 us (7%)
  matrix products  34.9 us (5%)
  starting transfers between devices  22.2 us (3%)
  between operations  14.9 us (2%)
    psum x1, waiting for transfers between devices, body(): lax.psum((grad_down, up_weight_gradient), ('dp', 'seq'))  229 us
    all_to_all x1, waiting for transfers between devices, body(): lax.all_to_all(sectioned, 'seq', split_axis=2, concat_axis=1, tiled=True)  74.3 us
    all_gather x1, waiting for transfers between devices, body(): incoming = lax.all_gather(attended, 'seq', axis=1, tiled=True)  66.1 us
    concatenate x2, local copies, waits for them, and re-layouts, body(): arrived = jnp.concatenate(pieces, axis=1)  31.1 us
    all_to_all x1, waiting for transfers between devices, body(): lax.all_to_all(mixed_cols, 'seq', split_axis=0, concat_axis=1, tiled=True)  29.5 us
    ppermute x5, waiting for transfers between devices, from_partner(): return lax.ppermute(block, axis, route)  26.5 us
    gather x5, local copies, waits for them, and re-layouts, body(): jnp.take(attention_inputs, jnp.minimum(start_row + slot_range, source_row...  20 us
  transfers between devices with their start and end apart: 9, of which 6 were waited for; matrix products, arithmetic and copies ran while one was open for 8% of the time, Pallas kernels for 0%

commit v1 on v0

v1 whole, which is shorter than its diff:
```python
import functools
import math

import jax
import jax.numpy as jnp
import numpy as np
from jax import lax
from jax.experimental import pallas as pl
from jax.experimental.pallas import tpu as pltpu
from jax.sharding import PartitionSpec as P

HEAD = 128
SLOT = 64
ADAPTER_SCALE = 2.0
FAR = (4, 5)
STREAMS = 4
VMEM_BYTES = 56 * 1024 * 1024
F32 = jnp.float32
BF16 = jnp.bfloat16


def contract(left, right, left_dim, right_dim):
    return lax.dot_general(
        left, right, (((left_dim,), (right_dim,)), ((), ())), preferred_element_type=F32
    )


def inverse_frequencies():
    sixth = HEAD // 6
    parts = []
    for width in (HEAD - 4 * sixth, 2 * sixth, 2 * sixth):
        exponent = np.arange(0, width, 2).astype(np.float32) / np.float32(width)
        parts.append(np.power(np.float32(10000.0), -exponent).astype(np.float32))
    return np.broadcast_to(np.repeat(np.concatenate(parts), 2)[None, :], (8, HEAD)).copy()


def iota(shape, dim):
    return lax.broadcasted_iota(jnp.int32, shape, dim)


def my_clips(table, group):
    def step(c, found):
        source, target = table[c, 0], table[c, 1]
        height, width = table[c, 3], table[c, 4]
        portion = table[c, 2] * height * width // 8
        is_source, is_target = source == group, target == group
        chosen = (
            is_source & is_target,
            is_source & jnp.logical_not(is_target),
            is_target & jnp.logical_not(is_source),
        )
        mine = (c, portion, height, width)
        return tuple(
            tuple(jnp.where(hit, new, old) for new, old in zip(mine, clip))
            for hit, clip in zip(chosen, found)
        )

    zero = jnp.int32(0)
    blank = tuple((zero, zero, jnp.int32(1), jnp.int32(1)) for _ in range(3))
    return lax.fori_loop(0, table.shape[0], step, blank)


def placement(shape, row_dim, first, second):
    row = iota(shape, row_dim)
    slot_row = iota(shape, 1 - row_dim)
    in_second = slot_row >= SLOT
    token = jnp.where(in_second, slot_row - SLOT, slot_row)
    offset = jnp.where(in_second, second[0], first[0])
    portion = jnp.where(in_second, second[1], first[1])
    return jnp.where((row == token + offset) & (token < portion), 1.0, 0.0).astype(BF16)


def prepare(place, table, frequency, rows, cotangent, up, *outs):
    stay_out, move_out, to_rows, info = outs
    group, shard = place[0], place[1]
    stay, leave, arrive = my_clips(table, group)
    zero = jnp.int32(0)
    leave_offset = jnp.where(stay[0] < leave[0], stay[1], zero)
    stay_offset = jnp.where(leave[0] < stay[0], leave[1], zero)
    arrive_target = jnp.where(stay[0] < arrive[0], stay[1], zero)
    stay_target = jnp.where(arrive[0] < stay[0], arrive[1], zero)
    info[0] = stay[1]
    info[1] = arrive[1]
    count = rows.shape[1]
    select = placement(
        (2 * SLOT, count), 1, (stay_offset, stay[1]), (leave_offset, leave[1])
    )
    target_rows = placement(
        (cotangent.shape[0], 2 * SLOT), 0, (stay_target, stay[1]), (arrive_target, arrive[1])
    )
    to_rows[...] = target_rows

    shape = (2 * SLOT, HEAD)
    slot_row = iota(shape, 0)
    in_second = slot_row >= SLOT
    token = jnp.where(in_second, slot_row - SLOT, slot_row)
    portion = jnp.where(in_second, leave[1], stay[1])
    height = jnp.where(in_second, leave[2], stay[2]).astype(F32)
    width = jnp.where(in_second, leave[3], stay[3]).astype(F32)
    token = (token + shard * portion).astype(F32)
    row_of = jnp.floor((token + 0.5) / width)
    frame = jnp.floor((token + 0.5) / (height * width))
    sixth = HEAD // 6
    lane = iota(shape, 1)
    position = jnp.where(
        lane < HEAD - 4 * sixth,
        frame,
        jnp.where(lane < HEAD - 2 * sixth, row_of - frame * height, token - row_of * width),
    )
    angle = position * frequency[0:1, :]
    cosine, sine = jnp.cos(angle), jnp.sin(angle)
    even = lane % 2 == 0
    sine_next, sine_last = jnp.where(even, -sine, 0.0), jnp.where(even, 0.0, sine)

    low = (ADAPTER_SCALE * contract(up[...], cotangent[...], 1, 1)).astype(BF16)
    low = contract(low, target_rows, 1, 0).astype(BF16)
    half = low.shape[0] // 2

    width_dev = stay_out.shape[2]
    for k in range(8):
        column = k * width_dev
        for part in range(3):
            placed = contract(select, rows[part, :, pl.ds(column, width_dev)], 1, 0)
            if part < 2:
                turned = []
                for head in range(width_dev // HEAD):
                    lanes = slice(head * HEAD, (head + 1) * HEAD)
                    mine = placed[:, lanes]
                    turned.append(
                        mine * cosine
                        + pltpu.roll(mine, HEAD - 1, 1) * sine_next
                        + pltpu.roll(mine, 1, 1) * sine_last
                    )
                placed = jnp.concatenate(turned, axis=1)
            placed = placed.astype(BF16)
            stay_out[k, part * SLOT : (part + 1) * SLOT, :] = placed[:SLOT]
            start = (3 * k + part) * SLOT
            move_out[start : start + SLOT, :] = placed[SLOT:]
        stay_out[k, 3 * SLOT : 3 * SLOT + half, 0:HEAD] = low[:half]
        stay_out[k, 3 * SLOT : 3 * SLOT + half, HEAD : 2 * HEAD] = low[half:]
        stay_out[k, 3 * SLOT : 3 * SLOT + half, 2 * HEAD :] = jnp.zeros(
            (half, width_dev - 2 * HEAD), BF16
        )


def clip_attention(blocks, portion, store):
    width_dev = blocks[0].shape[1]
    total = 8 * SLOT
    scale = 1.0 / math.sqrt(HEAD)
    valid = lax.rem(iota((total, total), 1), SLOT) < portion
    for head in range(width_dev // HEAD):
        lanes = slice(head * HEAD, (head + 1) * HEAD)
        query, key, value = (
            jnp.concatenate(
                [blocks[k][part * SLOT : (part + 1) * SLOT, lanes] for k in range(8)], axis=0
            )
            for part in range(3)
        )
        scores = jnp.where(valid, contract(query, key, 1, 1) * scale, -1e30)
        largest = jnp.max(scores, axis=1, keepdims=True)
        weights = jnp.exp(scores - largest)
        weights = (weights / jnp.sum(weights, axis=1, keepdims=True)).astype(BF16)
        store(lanes, contract(weights, value, 1, 0).astype(BF16))


def attend_first(info, blocks, out):
    blocks = [blocks.at[k] for k in range(8)]

    def store(lanes, result):
        out[:, lanes] = result

    clip_attention(blocks, info[0], store)


def attend_second(info, first, extras, blocks, out, gradient, second):
    blocks = [blocks.at[k] for k in range(8)]

    def store(lanes, result):
        second[:, lanes] = result

    clip_attention(blocks, info[1], store)
    gradient_sum = jnp.zeros(gradient.shape, F32)
    half = gradient.shape[0] // 2
    for k in range(8):
        rows = slice(k * SLOT, (k + 1) * SLOT)
        out[k, :SLOT, :] = first[rows, :]
        out[k, SLOT:, :] = second[rows, :]
        extra = extras[k, 3 * SLOT : 3 * SLOT + half, :]
        low = jnp.concatenate([extra[:, 0:HEAD], extra[:, HEAD : 2 * HEAD]], axis=0)
        gradient_sum += contract(low, out[k], 1, 0)
    gradient[...] = gradient_sum


def up_gradient(back, to_rows, down, cotangent, down_part, attended, adapted_out, part_out, wide):
    width_dev = back.shape[2]
    for k in range(8):
        attended[:, k * width_dev : (k + 1) * width_dev] = contract(
            to_rows[...], back[k], 1, 0
        ).astype(BF16)
    adapted = contract(down[...], attended[...], 1, 1).astype(BF16)
    adapted_out[...] = adapted
    result = ADAPTER_SCALE * contract(adapted, cotangent[...], 1, 0)
    tiles = result.shape[1] // HEAD
    for j in range(tiles):
        wide[:, j, :] = result[:, j * HEAD : (j + 1) * HEAD]
    for j in range(down_part.shape[1] // HEAD):
        wide[:, tiles + j, :] = down_part[:, j * HEAD : (j + 1) * HEAD]
    for j in range(tiles + down_part.shape[1] // HEAD, wide.shape[1]):
        wide[:, j, :] = jnp.zeros((wide.shape[0], HEAD), F32)
    part_out[...] = wide[...].astype(BF16)


def add_and_repeat(parts, out):
    total = parts[0].astype(F32)
    for i in range(1, parts.shape[0]):
        total += parts[i].astype(F32)
    out[...] = jnp.broadcast_to(total[None], out.shape)


def join_and_repeat(tiles, parts, out, row):
    row[0:tiles, :] = jnp.sum(parts[:, 0:tiles, :], axis=0)
    each = (row.shape[0] - tiles) // 8
    for block in range(8):
        row[tiles + each * block : tiles + each * (block + 1), :] = parts[
            block, tiles : tiles + each, :
        ]
    out[...] = jnp.broadcast_to(row[...].astype(BF16)[None], out.shape)


def spread(parts, up_out, down_out, wide):
    wide[...] = parts[...].astype(F32)
    tiles = up_out.shape[1] // HEAD
    for j in range(tiles):
        up_out[:, j * HEAD : (j + 1) * HEAD] = wide[:, j, :]
    for j in range(down_out.shape[1] // HEAD):
        down_out[:, j * HEAD : (j + 1) * HEAD] = wide[:, tiles + j, :]


def project_own(shard, attended, adapted, up, own, out):
    extra = ADAPTER_SCALE * contract(adapted[...], up[...], 0, 0)
    out[...] = (contract(attended[...], own[...], 1, 0) + extra).astype(BF16)


def project(shard, attended, adapted, up, *refs):
    total = ADAPTER_SCALE * contract(adapted[...], up[...], 0, 0)
    depth = refs[0].shape[0] * refs[0].shape[1]
    for i in range(STREAMS):
        block = refs[i][...].reshape(depth, refs[i].shape[2])
        total += contract(attended[:, i * depth : (i + 1) * depth], block, 1, 0)
    refs[-1][...] = total.astype(BF16)


VM = pl.BlockSpec(memory_space=pltpu.VMEM)
SM = pl.BlockSpec(memory_space=pltpu.SMEM)


def call(kernel, in_specs, out_shapes, out_specs=None, flops=0, size=0, scratch=()):
    return pl.pallas_call(
        kernel,
        in_specs=in_specs,
        out_shape=out_shapes,
        out_specs=out_specs if out_specs is not None else jax.tree.map(lambda _: VM, out_shapes),
        scratch_shapes=scratch,
        compiler_params=pltpu.CompilerParams(vmem_limit_bytes=VMEM_BYTES),
        cost_estimate=pl.CostEstimate(flops=flops, bytes_accessed=size, transcendentals=0),
    )


def body(clip_table, attention_inputs, out_weight, adapter_down, adapter_up_weight, cotangent):
    dp_count, seq_count = lax.axis_size("dp"), lax.axis_size("seq")
    group, shard = lax.axis_index("dp"), lax.axis_index("seq")
    features = attention_inputs.shape[2]
    width_dev = features // seq_count
    feature_dev = out_weight.shape[1]
    rank, model = adapter_up_weight.shape
    rows_dev = cotangent.shape[0]
    place = jnp.stack([group, shard]).astype(jnp.int32)
    struct = jax.ShapeDtypeStruct

    def turn(block, k):
        return lax.ppermute(block, "seq", [(i, (i + k) % seq_count) for i in range(seq_count)])

    weight_rows = features // dp_count
    own_rows = lax.dynamic_slice_in_dim(out_weight, group * weight_rows, weight_rows, 0)
    near = {k: turn(own_rows, -k) for k in range(1, seq_count) if k not in FAR}

    prepared = call(
        prepare,
        [SM, SM, VM, VM, VM, VM],
        [
            struct((seq_count, 3 * SLOT + rank // 2, width_dev), BF16),
            struct((seq_count * 3 * SLOT, width_dev), BF16),
            struct((rows_dev, 2 * SLOT), BF16),
            struct((2,), jnp.int32),
        ],
        [VM] * 3 + [SM],
        flops=10**9,
        size=6 * 10**6,
    )(
        place,
        clip_table,
        jnp.asarray(inverse_frequencies()),
        attention_inputs,
        cotangent,
        adapter_up_weight,
    )
    stay, moving, to_rows, info = prepared

    def exchange(block, axis):
        return lax.all_to_all(block, axis, split_axis=0, concat_axis=0, tiled=True)

    apart = jnp.max(jnp.bitwise_xor(clip_table[:, 0], clip_table[:, 1]))
    bits = dp_count.bit_length() - 1
    branch = sum((apart > (1 << b)).astype(jnp.int32) for b in range(bits - 1))

    def move(bit, moving, stay, above, below):
        moved = lax.ppermute(moving, "dp", [(g, g ^ (1 << bit)) for g in range(dp_count)])
        return moved, exchange(stay, "seq"), turn(above, -1), turn(below, 1)

    moving, *blocks = lax.optimization_barrier((moving, *near.values()))
    blocks = dict(zip(near, blocks))
    moved, stay, *far = lax.switch(
        branch,
        [functools.partial(move, bit) for bit in range(bits)],
        moving,
        stay,
        blocks[FAR[0] - 1],
        blocks[FAR[1] + 1],
    )
    blocks |= dict(zip(FAR, far))
    others = jnp.concatenate([blocks[k] for k in range(1, seq_count)], axis=0)
    others, moved, stay = lax.optimization_barrier((others, moved, stay))
    gathered = lax.all_gather(others, "dp", axis=0, tiled=True)
    gathered = gathered.reshape(dp_count, seq_count - 1, weight_rows, feature_dev)
    moved = exchange(moved.reshape(seq_count, 3 * SLOT, width_dev), "seq")
    first = call(
        attend_first,
        [SM, VM],
        struct((seq_count * SLOT, width_dev), BF16),
        VM,
        flops=10**9,
        size=2 * 10**6,
    )(info, stay)
    attended, down_part = call(
        attend_second,
        [SM] + [VM] * 3,
        [struct((seq_count, 2 * SLOT, width_dev), BF16), struct((rank, width_dev), F32)],
        flops=10**9,
        size=4 * 10**6,
        scratch=[pltpu.VMEM((seq_count * SLOT, width_dev), BF16)],
    )(info, first, stay, moved)
    back = exchange(attended, "seq")

    up_tiles, down_tiles = model // HEAD, features // HEAD
    piece_tiles = -(-(up_tiles + down_tiles // seq_count) // 16) * 16
    attended_rows, adapted, mine = call(
        up_gradient,
        [VM] * 5,
        [
            struct((rows_dev, features), BF16),
            struct((rank, rows_dev), BF16),
            struct((rank, piece_tiles, HEAD), BF16),
        ],
        flops=10**8,
        size=2 * 10**6,
        scratch=[pltpu.VMEM((rank, piece_tiles, HEAD), F32)],
    )(back, to_rows, adapter_down.T, cotangent, down_part)
    mine = exchange(mine, "dp")
    mine = call(add_and_repeat, [VM], struct((seq_count, piece_tiles, HEAD), F32), VM)(mine)

    def whole(shape):
        return pl.BlockSpec(shape, lambda k, s: (0,) * len(shape))

    def mixed_block(first_step):
        return lambda k, s: (0, lax.rem(s[0] + k + first_step, 8))

    begun = pl.pallas_call(
        project_own,
        grid_spec=pltpu.PrefetchScalarGridSpec(
            num_scalar_prefetch=1,
            grid=(1,),
            in_specs=[
                whole((rows_dev, features)),
                whole((rank, rows_dev)),
                pl.BlockSpec((rank, feature_dev), mixed_block(0)),
                whole((features, feature_dev)),
            ],
            out_specs=pl.BlockSpec((rows_dev, feature_dev), mixed_block(0)),
        ),
        out_shape=struct((rows_dev, model), BF16),
        compiler_params=pltpu.CompilerParams(vmem_limit_bytes=VMEM_BYTES),
        cost_estimate=pl.CostEstimate(
            flops=2 * rows_dev * features * feature_dev,
            bytes_accessed=2 * features * feature_dev,
            transcendentals=0,
        ),
    )(place[1:], attended_rows, adapted, adapter_up_weight, out_weight)

    mine = exchange(mine, "seq")
    mine = call(
        functools.partial(join_and_repeat, up_tiles),
        [VM],
        struct((dp_count, up_tiles + down_tiles, HEAD), BF16),
        VM,
        scratch=[pltpu.VMEM((up_tiles + down_tiles, HEAD), F32)],
    )(mine)
    mine, begun, gathered = lax.optimization_barrier((mine, begun, gathered))
    mine = exchange(mine, "dp")
    up_gradient_sum, down_gradient = call(
        spread,
        [VM],
        [struct((rank, model), F32), struct((rank, features), F32)],
        scratch=[pltpu.VMEM((dp_count, up_tiles + down_tiles, HEAD), F32)],
    )(mine)

    mixed = pl.pallas_call(
        project,
        grid_spec=pltpu.PrefetchScalarGridSpec(
            num_scalar_prefetch=1,
            grid=(seq_count - 1,),
            in_specs=[
                whole((rows_dev, features)),
                whole((rank, rows_dev)),
                pl.BlockSpec((rank, feature_dev), mixed_block(1)),
            ]
            + [
                pl.BlockSpec(
                    (dp_count // STREAMS, None, weight_rows, feature_dev),
                    lambda k, s, i=i: (i, k, 0, 0),
                )
                for i in range(STREAMS)
            ]
            + [pl.BlockSpec(memory_space=pl.ANY)],
            out_specs=pl.BlockSpec((rows_dev, feature_dev), mixed_block(1)),
        ),
        out_shape=struct((rows_dev, model), BF16),
        input_output_aliases={4 + STREAMS: 0},
        compiler_params=pltpu.CompilerParams(vmem_limit_bytes=VMEM_BYTES),
        cost_estimate=pl.CostEstimate(
            flops=2 * rows_dev * features * model,
            bytes_accessed=2 * features * model,
            transcendentals=0,
        ),
    )(place[1:], attended_rows, adapted, adapter_up_weight, *[gathered] * STREAMS, begun)
    return (mixed, down_gradient.T, up_gradient_sum)


def solution(mesh):
    in_specs = (P(), P(None, ("dp", "seq"), None), P(None, "seq"), P(), P(), P(("dp", "seq"), None))
    out_specs = (P(("dp", "seq"), None), P(), P())
    return jax.shard_map(body, mesh=mesh, in_specs=in_specs, out_specs=out_specs, check_vma=False)
```

time: 660 us -> 219 us (0.33); the launches traced: 651 us -> 218 us
  waiting for transfers between devices: 425 us -> 61.3 us
  local copies, waits for them, and re-layouts: 107 us -> 7.64 us
  blocking collectives: 0 us -> 49.1 us
  other arithmetic: 46.9 us -> 1.98 us
  Pallas kernels: 0 us -> 43 us
  matrix products: 34.9 us -> 0 us
  starting transfers between devices: 22.2 us -> 37.9 us
    psum x1 -> x0, waiting for transfers between devices: 229 us -> none  [body(): lax.psum((grad_down, up_weight_gradient), ('dp', 'seq'))]
    all_to_all x2 -> x4, waiting for transfers between devices: 104 us -> 35.1 us  [exchange(): return lax.all_to_all(block, axis, split_axis=0, concat_axis=0, tiled=True)]
    all_gather x1, waiting for transfers between devices: 66.1 us -> 0.01 us  [body(): gathered = lax.all_gather(others, 'dp', axis=0, tiled=True)]
    all_to_all x0 -> x2, blocking collectives: none -> 49.1 us  [exchange(): return lax.all_to_all(block, axis, split_axis=0, concat_axis=0, tiled=True)]
    pallas_call x0 -> x9, Pallas kernels: none -> 43 us  [the longest x1 13.5 us: body(): pl.pallas_call(project, grid_spec=pltpu.PrefetchScalarGridSpec(num_scalar...]
    dot_general x13 -> x0, matrix products: 34.9 us -> none  [the longest x3 10.3 us: body(): jnp.dot(queries[:, head_number], rotated_keys[:, head_number].T, preferre...]
    gather x7 -> x0, local copies, waits for them, and re-layouts: 32.4 us -> none  [the longest x5 20 us: body(): jnp.take(attention_inputs, jnp.minimum(start_row + slot_range, source_row...]
    concatenate x2 -> x1, local copies, waits for them, and re-layouts: 31.1 us -> 0.02 us  [body(): others = jnp.concatenate([blocks[k] for k in range(1, seq_count)], axis=0)]
  transfers between devices with their start and end apart: 9 -> 13, of which waited for: 6 -> 5; matrix products, arithmetic and copies ran while one was open for 8% -> 2% of each run, Pallas kernels for 0% -> 19%
where the time goes in v1:
time: 219 us; the launch traced here: 218 us
  waiting for transfers between devices  61.3 us (28%)
  blocking collectives  49.1 us (22%)
  Pallas kernels  43 us (20%)
  starting transfers between devices  37.9 us (17%)
  between operations  16.7 us (8%)
  local copies, waits for them, and re-layouts  7.64 us (3%)
    all_to_all x2, blocking collectives, exchange(): return lax.all_to_all(block, axis, split_axis=0, concat_axis=0, tiled=True)  49.1 us
    all_to_all x4, waiting for transfers between devices, exchange(): return lax.all_to_all(block, axis, split_axis=0, concat_axis=0, tiled=True)  35.1 us
    ppermute x7, waiting for transfers between devices, turn(): lax.ppermute(block, 'seq', [(i, (i + k) % seq_count) for i in range(seq_c...  26.2 us
    all_to_all x4, starting transfers between devices, exchange(): return lax.all_to_all(block, axis, split_axis=0, concat_axis=0, tiled=True)  20.1 us
    ppermute x7, starting transfers between devices, turn(): lax.ppermute(block, 'seq', [(i, (i + k) % seq_count) for i in range(seq_c...  15.1 us
    pallas_call x1, Pallas kernels, body(): pl.pallas_call(project, grid_spec=pltpu.PrefetchScalarGridSpec(num_scalar...  13.5 us
    pallas_call x1, Pallas kernels, body(): call(prepare, [SM, SM, VM, VM, VM, VM], [struct((seq_count, 3 * SLOT + ra...  7.3 us
    unnamed x15, local copies, waits for them, and re-layouts  6.7 us
  transfers between devices with their start and end apart: 13, of which 5 were waited for; matrix products, arithmetic and copies ran while one was open for 2% of the time, Pallas kernels for 19%

profile of v1, /device:TPU:1, one launch (start us, length us, event | category | flops | bytes accessed | tf_op | source)
XLA Modules:
  0.0 217.7 jit_solution(16623044910622244436)
XLA Ops:
  8.1 2.5 %collective-permute-start.19 = (bf16[96,640]{1,0:T(8,128)(2,1)S(1)}, bf16[96,640]{1,0:T(8,128)(2,1)S(1)}, u32[]{:S(2)}, u32[]{:S(2)}) collective-permute-start(bf16[96,640]{1,0:T(8,128)(2,1)S(1)} %constant_dynamic-slice_fusion), channel_id=1, source_target_pairs={{0,1},{1,2},{2,3},{3,4},{4,5},{5,6},{6,7},{7,0},{8,9},{9,10},{10,1... | collective-permute-start | bytes 368648 | tf_op jit(solution)/shard_map/ppermute | solution.py:281
  10.7 3.0 %collective-permute-start.18 = (bf16[96,640]{1,0:T(8,128)(2,1)S(1)}, bf16[96,640]{1,0:T(8,128)(2,1)S(1)}, u32[]{:S(2)}, u32[]{:S(2)}) collective-permute-start(bf16[96,640]{1,0:T(8,128)(2,1)S(1)} %constant_dynamic-slice_fusion), channel_id=1, source_target_pairs={{0,2},{1,3},{2,4},{3,5},{4,6},{5,7},{6,0},{7,1},{8,10},{9,11},{10,... | collective-permute-start | bytes 368648 | tf_op jit(solution)/shard_map/ppermute | solution.py:281
  13.7 3.1 %collective-permute-start.17 = (bf16[96,640]{1,0:T(8,128)(2,1)S(1)}, bf16[96,640]{1,0:T(8,128)(2,1)S(1)}, u32[]{:S(2)}, u32[]{:S(2)}) collective-permute-start(bf16[96,640]{1,0:T(8,128)(2,1)S(1)} %constant_dynamic-slice_fusion), channel_id=1, source_target_pairs={{0,5},{1,6},{2,7},{3,0},{4,1},{5,2},{6,3},{7,4},{8,13},{9,14},{10,... | collective-permute-start | bytes 368648 | tf_op jit(solution)/shard_map/ppermute | solution.py:281
  16.8 3.0 %collective-permute-start.16 = (bf16[96,640]{1,0:T(8,128)(2,1)S(1)}, bf16[96,640]{1,0:T(8,128)(2,1)S(1)}, u32[]{:S(2)}, u32[]{:S(2)}) collective-permute-start(bf16[96,640]{1,0:T(8,128)(2,1)S(1)} %constant_dynamic-slice_fusion), channel_id=1, source_target_pairs={{0,6},{1,7},{2,0},{3,1},{4,2},{5,3},{6,4},{7,5},{8,14},{9,15},{10,... | collective-permute-start | bytes 368648 | tf_op jit(solution)/shard_map/ppermute | solution.py:281
  26.5 7.3 %shard_map.94 = (bf16[8,208,384]{2,1,0:T(8,128)(2,1)}, bf16[1536,384]{1,0:T(8,128)(2,1)S(1)}, bf16[128,128]{1,0:T(8,128)(2,1)}, s32[2]{0:T(128)}) custom-call(s32[2]{0:T(128)} %pad_add_fusion.place, s32[64,5]{1,0:T(8,128)} %copy.11.table, f32[8,128]{1,0:T(8,128)} %constant.27.clone.frequency, bf16[3,128,3072]{2,1,0:T(8,128)(2,1)} %rows.1, ...), custom_call_target="tpu_custom_call" | custom-call | flops 1000000000 | bytes 6000000 | tf_op jit(solution)/shard_map/pallas_call | solution.py:287
  34.0 39.4 %conditional.1 = (bf16[1536,384]{1,0:T(8,128)(2,1)}, bf16[8,208,384]{2,1,0:T(8,128)(2,1)}, bf16[96,640]{1,0:T(8,128)(2,1)}, bf16[96,640]{1,0:T(8,128)(2,1)}) conditional(s32[]{:T(128)} %clamp.3, (bf16[1536,384]{1,0:T(8,128)(2,1)S(1)}, bf16[8,208,384]{2,1,0:T(8,128)(2,1)}, bf16[96,640]{1,0:T(8,128)(2,1)S(1)}, ...), branch_computations={%region_1.0_spmd, %region_2.0_spmd, %region_3.0_spmd, %region_4.0_... | conditional | bytes 9535672 | solution.py:322
  34.0 5.1 %all-to-all-start.2 = ((bf16[8,208,384]{2,1,0:T(8,128)(2,1)}), bf16[8,208,384]{2,1,0:T(8,128)(2,1)}, u32[]{:S(2)}, u32[]{:S(2)}) async-start(bf16[8,208,384]{2,1,0:T(8,128)(2,1)} %get-tuple-element.49), calls=%async_computation.2 | async-start | bytes 2555904 | tf_op jit(solution)/shard_map/cond/branch_2_fun/all_to_all | solution.py:310
  39.1 2.7 %collective-permute-start.6 = (bf16[1536,384]{1,0:T(8,128)(2,1)S(1)}, bf16[1536,384]{1,0:T(8,128)(2,1)}, u32[]{:S(2)}, u32[]{:S(2)}) collective-permute-start(bf16[1536,384]{1,0:T(8,128)(2,1)S(1)} %get-tuple-element.48), channel_id=1, source_target_pairs={{0,32},{8,40},{16,48},{24,56},{32,0},{40,8},{48,16},{56,24},{64,96... | collective-permute-start | bytes 3538952 | tf_op jit(solution)/shard_map/cond/branch_2_fun/ppermute | solution.py:317
  41.8 2.7 %collective-permute-start.7 = (bf16[96,640]{1,0:T(8,128)(2,1)S(1)}, bf16[96,640]{1,0:T(8,128)(2,1)}, u32[]{:S(2)}, u32[]{:S(2)}) collective-permute-start(bf16[96,640]{1,0:T(8,128)(2,1)S(1)} %get-tuple-element.50), channel_id=1, source_target_pairs={{0,7},{1,0},{2,1},{3,2},{4,3},{5,4},{6,5},{7,6},{8,15},{9,8},{10,9... | collective-permute-start | bytes 368648 | tf_op jit(solution)/shard_map/cond/branch_2_fun/ppermute | solution.py:281
  44.5 25.5 %collective-permute-done.7 = bf16[96,640]{1,0:T(8,128)(2,1)} collective-permute-done((bf16[96,640]{1,0:T(8,128)(2,1)S(1)}, bf16[96,640]{1,0:T(8,128)(2,1)}, u32[]{:S(2)}, u32[]{:S(2)}) %collective-permute-start.7) | collective-permute-done | bytes 122912 | tf_op jit(solution)/shard_map/cond/branch_2_fun/ppermute | solution.py:281
  70.7 2.7 %all-to-all-done.2 = bf16[8,208,384]{2,1,0:T(8,128)(2,1)} async-done(((bf16[8,208,384]{2,1,0:T(8,128)(2,1)}), bf16[8,208,384]{2,1,0:T(8,128)(2,1)}, u32[]{:S(2)}, u32[]{:S(2)}) %all-to-all-start.2) | async-done | bytes 1277984 | tf_op jit(solution)/shard_map/cond/branch_2_fun/all_to_all | solution.py:310
  76.2 4.2 %all-to-all-start.5 = ((bf16[8,192,384]{2,1,0:T(8,128)(2,1)}), bf16[8,192,384]{2,1,0:T(8,128)(2,1)S(1)}, u32[]{:S(2)}, u32[]{:S(2)}) async-start(bf16[8,192,384]{2,1,0:T(8,128)(2,1)} %bitcast.2), calls=%async_computation.5 | async-start | bytes 2359296 | tf_op jit(solution)/shard_map/all_to_all | solution.py:310
  80.4 3.8 %shard_map.95.first = bf16[512,384]{1,0:T(8,128)(2,1)} custom-call(s32[2]{0:T(128)} %get-tuple-element.90.info, bf16[8,208,384]{2,1,0:T(8,128)(2,1)} %get-tuple-element.103.blocks.extras), custom_call_target="tpu_custom_call" | custom-call | flops 1000000000 | bytes 2000000 | tf_op jit(solution)/shard_map/pallas_call | solution.py:336
  84.2 28.3 %all-to-all-done.5.blocks = bf16[8,192,384]{2,1,0:T(8,128)(2,1)S(1)} async-done(((bf16[8,192,384]{2,1,0:T(8,128)(2,1)}), bf16[8,192,384]{2,1,0:T(8,128)(2,1)S(1)}, u32[]{:S(2)}, u32[]{:S(2)}) %all-to-all-start.5) | async-done | bytes 1179680 | tf_op jit(solution)/shard_map/all_to_all | solution.py:310
  113.5 4.5 %shard_map.96 = (bf16[8,128,384]{2,1,0:T(8,128)(2,1)}, f32[32,384]{1,0:T(8,128)}) custom-call(s32[2]{0:T(128)} %get-tuple-element.90.info, bf16[512,384]{1,0:T(8,128)(2,1)} %shard_map.95.first, bf16[8,208,384]{2,1,0:T(8,128)(2,1)} %get-tuple-element.103.blocks.extras, bf16[8,192,384]{2,1,0:T(8,128)(2,1)} %copy-done.1), custom_call_target="tpu_custom_call" | custom-call | flops 1000000000 | bytes 4000000 | tf_op jit(solution)/shard_map/pallas_call | solution.py:344
  117.9 27.5 %all_to_all.45.back = bf16[8,128,384]{2,1,0:T(8,128)(2,1)} all-to-all(bf16[8,128,384]{2,1,0:T(8,128)(2,1)} %get-tuple-element.105), channel_id=1, replica_groups=mesh['dp'=32,'seq'=8] {'seq'}, dimensions={0} | all-to-all | bytes 1572864 | tf_op jit(solution)/shard_map/all_to_all | solution.py:310
  145.5 3.8 %shard_map.97 = (bf16[128,3072]{1,0:T(8,128)(2,1)}, bf16[32,128]{1,0:T(8,128)(2,1)}, bf16[32,48,128]{2,1,0:T(8,128)(2,1)}) custom-call(bf16[8,128,384]{2,1,0:T(8,128)(2,1)} %all_to_all.45.back, bf16[128,128]{1,0:T(8,128)(2,1)} %get-tuple-element.106.to_rows, bf16[32,3072]{1,0:T(8,128)(2,1)} %bitcast.10, bf16[128,5120]{1,0:T(8,128)(2,1)} %cotangent.3, ...), custom_call_target="tpu_custom_call" | custom-call | flops 100000000 | bytes 2000000 | tf_op jit(solution)/shard_map/pallas_call | solution.py:356
  149.3 21.5 %all_to_all.46.parts = bf16[32,48,128]{2,1,0:T(8,128)(2,1)} all-to-all(bf16[32,48,128]{2,1,0:T(8,128)(2,1)} %get-tuple-element.110), channel_id=1, replica_groups=mesh['dp'=32,'seq'=8] {'dp'}, dimensions={0} | all-to-all | bytes 786432 | tf_op jit(solution)/shard_map/all_to_all | solution.py:310
  172.6 3.4 %all-to-all-start.8 = ((f32[8,48,128]{2,1,0:T(8,128)}), f32[8,48,128]{2,1,0:T(8,128)S(1)}, u32[]{:S(2)}, u32[]{:S(2)}) async-start(f32[8,48,128]{2,1,0:T(8,128)} %shard_map.98), calls=%async_computation.8 | async-start | bytes 393216 | tf_op jit(solution)/shard_map/all_to_all | solution.py:310
  176.0 4.2 %shard_map.100.refs_4_ = bf16[128,5120]{1,0:T(8,128)(2,1)} custom-call(s32[1]{0:T(128)} %bitcast.shard, bf16[128,3072]{1,0:T(8,128)(2,1)} %get-tuple-element.108.attended, bf16[32,128]{1,0:T(8,128)(2,1)} %get-tuple-element.109.adapted, bf16[32,5120]{1,0:T(8,128)(2,1)} %up.5, bf16[3072,640]{1,0:T(8,128)(2,1)} %own.1), custom_call_target="tpu_custom_call" | custom-call | flops 503316480 | bytes 3932160 | tf_op jit(solution)/shard_map/pallas_call | solution.py:377
  180.2 4.1 %all-to-all-done.8.parts = f32[8,48,128]{2,1,0:T(8,128)S(1)} async-done(((f32[8,48,128]{2,1,0:T(8,128)}), f32[8,48,128]{2,1,0:T(8,128)S(1)}, u32[]{:S(2)}, u32[]{:S(2)}) %all-to-all-start.8) | async-done | bytes 196640 | tf_op jit(solution)/shard_map/all_to_all | solution.py:310
  186.7 7.4 %all-to-all-start.9 = ((bf16[32,64,128]{2,1,0:T(8,128)(2,1)}), bf16[32,64,128]{2,1,0:T(8,128)(2,1)S(1)}, u32[]{:S(2)}, u32[]{:S(2)}) async-start(bf16[32,64,128]{2,1,0:T(8,128)(2,1)} %shard_map.99), calls=%async_computation.9 | async-start | bytes 1048576 | tf_op jit(solution)/shard_map/all_to_all | solution.py:310
  194.1 13.5 %shard_map.101 = bf16[128,5120]{1,0:T(8,128)(2,1)} custom-call(s32[1]{0:T(128)} %bitcast.shard, bf16[128,3072]{1,0:T(8,128)(2,1)} %get-tuple-element.108.attended, bf16[32,128]{1,0:T(8,128)(2,1)} %get-tuple-element.109.adapted, bf16[32,5120]{1,0:T(8,128)(2,1)} %up.5, bf16[32,7,96,640]{3,2,1,0:T(8,128)(2,1)} %bitcast.6, ...), custom_call_target="tpu_custom_call", output_to_operand_aliasing={{}: (8, {})} | custom-call | flops 4026531840 | bytes 31457280 | tf_op jit(solution)/shard_map/pallas_call | solution.py:416
  208.4 2.5 %shard_map.102 = (f32[32,5120]{1,0:T(8,128)}, f32[32,3072]{1,0:T(8,128)}) custom-call(bf16[32,64,128]{2,1,0:T(8,128)(2,1)} %copy-done), custom_call_target="tpu_custom_call" | custom-call | tf_op jit(solution)/shard_map/pallas_call | solution.py:409
  (34 shorter events, 14.6 us)
Async XLA Ops:
  7.2 179.6 %all-gather.2.cloned.1.call-start = ((), (), s32[]{:S(2)}) async-start(), calls=%async_computation.10 | async-start | bytes 28385280 | tf_op jit(solution)/shard_map/all_gather | solution.py:333
  8.1 25.7 %collective-permute-start.19 = (bf16[96,640]{1,0:T(8,128)(2,1)S(1)}, bf16[96,640]{1,0:T(8,128)(2,1)S(1)}, u32[]{:S(2)}, u32[]{:S(2)}) collective-permute-start(bf16[96,640]{1,0:T(8,128)(2,1)S(1)} %constant_dynamic-slice_fusion), channel_id=1, source_target_pairs={{0,1},{1,2},{2,3},{3,4},{4,5},{5,6},{6,7},{7,0},{8,9},{9,10},{10,1... | collective-permute-start | bytes 368648 | tf_op jit(solution)/shard_map/ppermute | solution.py:281
  10.7 23.2 %collective-permute-start.18 = (bf16[96,640]{1,0:T(8,128)(2,1)S(1)}, bf16[96,640]{1,0:T(8,128)(2,1)S(1)}, u32[]{:S(2)}, u32[]{:S(2)}) collective-permute-start(bf16[96,640]{1,0:T(8,128)(2,1)S(1)} %constant_dynamic-slice_fusion), channel_id=1, source_target_pairs={{0,2},{1,3},{2,4},{3,5},{4,6},{5,7},{6,0},{7,1},{8,10},{9,11},{10,... | collective-permute-start | bytes 368648 | tf_op jit(solution)/shard_map/ppermute | solution.py:281
  13.7 20.2 %collective-permute-start.17 = (bf16[96,640]{1,0:T(8,128)(2,1)S(1)}, bf16[96,640]{1,0:T(8,128)(2,1)S(1)}, u32[]{:S(2)}, u32[]{:S(2)}) collective-permute-start(bf16[96,640]{1,0:T(8,128)(2,1)S(1)} %constant_dynamic-slice_fusion), channel_id=1, source_target_pairs={{0,5},{1,6},{2,7},{3,0},{4,1},{5,2},{6,3},{7,4},{8,13},{9,14},{10,... | collective-permute-start | bytes 368648 | tf_op jit(solution)/shard_map/ppermute | solution.py:281
  16.8 17.1 %collective-permute-start.16 = (bf16[96,640]{1,0:T(8,128)(2,1)S(1)}, bf16[96,640]{1,0:T(8,128)(2,1)S(1)}, u32[]{:S(2)}, u32[]{:S(2)}) collective-permute-start(bf16[96,640]{1,0:T(8,128)(2,1)S(1)} %constant_dynamic-slice_fusion), channel_id=1, source_target_pairs={{0,6},{1,7},{2,0},{3,1},{4,2},{5,3},{6,4},{7,5},{8,14},{9,15},{10,... | collective-permute-start | bytes 368648 | tf_op jit(solution)/shard_map/ppermute | solution.py:281
  19.8 14.1 %collective-permute-start.15 = (bf16[96,640]{1,0:T(8,128)(2,1)S(1)}, bf16[96,640]{1,0:T(8,128)(2,1)S(1)}, u32[]{:S(2)}, u32[]{:S(2)}) collective-permute-start(bf16[96,640]{1,0:T(8,128)(2,1)S(1)} %constant_dynamic-slice_fusion), channel_id=1, source_target_pairs={{0,7},{1,0},{2,1},{3,2},{4,3},{5,4},{6,5},{7,6},{8,15},{9,8},{10,9... | collective-permute-start | bytes 368648 | tf_op jit(solution)/shard_map/ppermute | solution.py:281
  34.0 39.3 %all-to-all-start.2 = ((bf16[8,208,384]{2,1,0:T(8,128)(2,1)}), bf16[8,208,384]{2,1,0:T(8,128)(2,1)}, u32[]{:S(2)}, u32[]{:S(2)}) async-start(bf16[8,208,384]{2,1,0:T(8,128)(2,1)} %get-tuple-element.49), calls=%async_computation.2 | async-start | bytes 2555904 | tf_op jit(solution)/shard_map/cond/branch_2_fun/all_to_all | solution.py:310
  39.1 31.6 %collective-permute-start.6 = (bf16[1536,384]{1,0:T(8,128)(2,1)S(1)}, bf16[1536,384]{1,0:T(8,128)(2,1)}, u32[]{:S(2)}, u32[]{:S(2)}) collective-permute-start(bf16[1536,384]{1,0:T(8,128)(2,1)S(1)} %get-tuple-element.48), channel_id=1, source_target_pairs={{0,32},{8,40},{16,48},{24,56},{32,0},{40,8},{48,16},{56,24},{64,96... | collective-permute-start | bytes 3538952 | tf_op jit(solution)/shard_map/cond/branch_2_fun/ppermute | solution.py:317
  41.8 28.2 %collective-permute-start.7 = (bf16[96,640]{1,0:T(8,128)(2,1)S(1)}, bf16[96,640]{1,0:T(8,128)(2,1)}, u32[]{:S(2)}, u32[]{:S(2)}) collective-permute-start(bf16[96,640]{1,0:T(8,128)(2,1)S(1)} %get-tuple-element.50), channel_id=1, source_target_pairs={{0,7},{1,0},{2,1},{3,2},{4,3},{5,4},{6,5},{7,6},{8,15},{9,8},{10,9... | collective-permute-start | bytes 368648 | tf_op jit(solution)/shard_map/cond/branch_2_fun/ppermute | solution.py:281
  44.5 26.2 %collective-permute-start.8 = (bf16[96,640]{1,0:T(8,128)(2,1)S(1)}, bf16[96,640]{1,0:T(8,128)(2,1)}, u32[]{:S(2)}, u32[]{:S(2)}) collective-permute-start(bf16[96,640]{1,0:T(8,128)(2,1)S(1)} %get-tuple-element.51), channel_id=1, source_target_pairs={{0,1},{1,2},{2,3},{3,4},{4,5},{5,6},{6,7},{7,0},{8,9},{9,10},{10,1... | collective-permute-start | bytes 368648 | tf_op jit(solution)/shard_map/cond/branch_2_fun/ppermute | solution.py:281
  75.3 0.9 copy-start.2
  76.2 36.3 %all-to-all-start.5 = ((bf16[8,192,384]{2,1,0:T(8,128)(2,1)}), bf16[8,192,384]{2,1,0:T(8,128)(2,1)S(1)}, u32[]{:S(2)}, u32[]{:S(2)}) async-start(bf16[8,192,384]{2,1,0:T(8,128)(2,1)} %bitcast.2), calls=%async_computation.5 | async-start | bytes 2359296 | tf_op jit(solution)/shard_map/all_to_all | solution.py:310
  112.5 1.0 copy-start.1
  172.6 11.7 %all-to-all-start.8 = ((f32[8,48,128]{2,1,0:T(8,128)}), f32[8,48,128]{2,1,0:T(8,128)S(1)}, u32[]{:S(2)}, u32[]{:S(2)}) async-start(f32[8,48,128]{2,1,0:T(8,128)} %shard_map.98), calls=%async_computation.8 | async-start | bytes 393216 | tf_op jit(solution)/shard_map/all_to_all | solution.py:310
  184.3 0.7 copy-start.3
  186.7 20.9 %all-to-all-start.9 = ((bf16[32,64,128]{2,1,0:T(8,128)(2,1)}), bf16[32,64,128]{2,1,0:T(8,128)(2,1)S(1)}, u32[]{:S(2)}, u32[]{:S(2)}) async-start(bf16[32,64,128]{2,1,0:T(8,128)(2,1)} %shard_map.99), calls=%async_computation.9 | async-start | bytes 1048576 | tf_op jit(solution)/shard_map/all_to_all | solution.py:310
  207.6 0.8 copy-start
Sparse Core Ops, SparseCore 0:
  76.3 106.9 all-gather.1

commit v2 on v1

--- a/solution.py
+++ b/solution.py
@@ -13,6 +13,7 @@
 SLOT = 64
 ADAPTER_SCALE = 2.0
 FAR = (4, 5)
+GATHERED = (1, 2, 3, 6, 7, 4, 5)
 STREAMS = 4
 VMEM_BYTES = 56 * 1024 * 1024
 F32 = jnp.float32
@@ -40,9 +41,9 @@
 
 def my_clips(table, group):
     def step(c, found):
-        source, target = table[c, 0], table[c, 1]
-        height, width = table[c, 3], table[c, 4]
-        portion = table[c, 2] * height * width // 8
+        source, target = table[0, c], table[1, c]
+        height, width = table[3, c], table[4, c]
+        portion = table[2, c] * height * width // 8
         is_source, is_target = source == group, target == group
         chosen = (
             is_source & is_target,
@@ -57,7 +58,7 @@
 
     zero = jnp.int32(0)
     blank = tuple((zero, zero, jnp.int32(1), jnp.int32(1)) for _ in range(3))
-    return lax.fori_loop(0, table.shape[0], step, blank)
+    return lax.fori_loop(0, table.shape[1], step, blank)
 
 
 def placement(shape, row_dim, first, second):
@@ -298,7 +299,7 @@
         size=6 * 10**6,
     )(
         place,
-        clip_table,
+        clip_table.T,
         jnp.asarray(inverse_frequencies()),
         attention_inputs,
         cotangent,
@@ -309,9 +310,9 @@
     def exchange(block, axis):
         return lax.all_to_all(block, axis, split_axis=0, concat_axis=0, tiled=True)
 
-    apart = jnp.max(jnp.bitwise_xor(clip_table[:, 0], clip_table[:, 1]))
+    apart = jnp.bitwise_xor(clip_table[:, 0], clip_table[:, 1])
     bits = dp_count.bit_length() - 1
-    branch = sum((apart > (1 << b)).astype(jnp.int32) for b in range(bits - 1))
+    branch = jnp.max(sum((apart > (1 << b)).astype(jnp.int32) for b in range(bits - 1)))
 
     def move(bit, moving, stay, above, below):
         moved = lax.ppermute(moving, "dp", [(g, g ^ (1 << bit)) for g in range(dp_count)])
@@ -328,7 +329,7 @@
         blocks[FAR[1] + 1],
     )
     blocks |= dict(zip(FAR, far))
-    others = jnp.concatenate([blocks[k] for k in range(1, seq_count)], axis=0)
+    others = jnp.concatenate([blocks[k] for k in GATHERED], axis=0)
     others, moved, stay = lax.optimization_barrier((others, moved, stay))
     gathered = lax.all_gather(others, "dp", axis=0, tiled=True)
     gathered = gathered.reshape(dp_count, seq_count - 1, weight_rows, feature_dev)
@@ -371,8 +372,12 @@
     def whole(shape):
         return pl.BlockSpec(shape, lambda k, s: (0,) * len(shape))
 
-    def mixed_block(first_step):
-        return lambda k, s: (0, lax.rem(s[0] + k + first_step, 8))
+    def own_block(k, s):
+        return (0, s[0])
+
+    def gathered_block(k, s):
+        away = jnp.where(k < 3, k + 1, jnp.where(k < 5, k + 3, k - 1))
+        return (0, lax.rem(s[0] + away, 8))
 
     begun = pl.pallas_call(
         project_own,
@@ -382,10 +387,10 @@
             in_specs=[
                 whole((rows_dev, features)),
                 whole((rank, rows_dev)),
-                pl.BlockSpec((rank, feature_dev), mixed_block(0)),
+                pl.BlockSpec((rank, feature_dev), own_block),
                 whole((features, feature_dev)),
             ],
-            out_specs=pl.BlockSpec((rows_dev, feature_dev), mixed_block(0)),
+            out_specs=pl.BlockSpec((rows_dev, feature_dev), own_block),
         ),
         out_shape=struct((rows_dev, model), BF16),
         compiler_params=pltpu.CompilerParams(vmem_limit_bytes=VMEM_BYTES),
@@ -421,7 +426,7 @@
             in_specs=[
                 whole((rows_dev, features)),
                 whole((rank, rows_dev)),
-                pl.BlockSpec((rank, feature_dev), mixed_block(1)),
+                pl.BlockSpec((rank, feature_dev), gathered_block),
             ]
             + [
                 pl.BlockSpec(
@@ -431,7 +436,7 @@
                 for i in range(STREAMS)
             ]
             + [pl.BlockSpec(memory_space=pl.ANY)],
-            out_specs=pl.BlockSpec((rows_dev, feature_dev), mixed_block(1)),
+            out_specs=pl.BlockSpec((rows_dev, feature_dev), gathered_block),
         ),
         out_shape=struct((rows_dev, model), BF16),
         input_output_aliases={4 + STREAMS: 0},

time: 219 us -> 219 us (level)
  waiting for transfers between devices: 61.3 us -> 64.5 us
    ppermute x7, waiting for transfers between devices: 26.2 us -> 29.5 us  [turn(): lax.ppermute(block, 'seq', [(i, (i + k) % seq_count) for i in range(seq_c...]
    unnamed x15 -> x14, local copies, waits for them, and re-layouts: 6.7 us -> 4.41 us
  transfers between devices with their start and end apart: 13 -> 13, of which waited for: 5 -> 6; matrix products, arithmetic and copies ran while one was open for 2% -> 1% of each run, Pallas kernels for 19% -> 19%
where the time goes in v2:
time: 219 us; the launch traced here: 218 us
  waiting for transfers between devices  64.5 us (29%)
  blocking collectives  49.1 us (22%)
  Pallas kernels  43.1 us (20%)
  starting transfers between devices  37.9 us (17%)
  between operations  14.8 us (7%)
  local copies, waits for them, and re-layouts  6.25 us (3%)
    all_to_all x2, blocking collectives, exchange(): return lax.all_to_all(block, axis, split_axis=0, concat_axis=0, tiled=True)  49.1 us
    all_to_all x4, waiting for transfers between devices, exchange(): return lax.all_to_all(block, axis, split_axis=0, concat_axis=0, tiled=True)  35.1 us
    ppermute x7, waiting for transfers between devices, turn(): lax.ppermute(block, 'seq', [(i, (i + k) % seq_count) for i in range(seq_c...  29.5 us
    all_to_all x4, starting transfers between devices, exchange(): return lax.all_to_all(block, axis, split_axis=0, concat_axis=0, tiled=True)  20 us
    ppermute x7, starting transfers between devices, turn(): lax.ppermute(block, 'seq', [(i, (i + k) % seq_count) for i in range(seq_c...  15.1 us
    pallas_call x1, Pallas kernels, body(): pl.pallas_call(project, grid_spec=pltpu.PrefetchScalarGridSpec(num_scalar...  13.5 us
    pallas_call x1, Pallas kernels, body(): call(prepare, [SM, SM, VM, VM, VM, VM], [struct((seq_count, 3 * SLOT + ra...  7.4 us
    pallas_call x1, Pallas kernels, body(): call(attend_second, [SM] + [VM] * 3, [struct((seq_count, 2 * SLOT, width_...  4.47 us
  transfers between devices with their start and end apart: 13, of which 6 were waited for; matrix products, arithmetic and copies ran while one was open for 1% of the time, Pallas kernels for 19%

profile of v2, /device:TPU:1, one launch (start us, length us, event | category | flops | bytes accessed | tf_op | source)
XLA Modules:
  0.0 217.7 jit_solution(14579885440004122826)
XLA Ops:
  8.1 2.5 %collective-permute-start.19 = (bf16[96,640]{1,0:T(8,128)(2,1)S(1)}, bf16[96,640]{1,0:T(8,128)(2,1)S(1)}, u32[]{:S(2)}, u32[]{:S(2)}) collective-permute-start(bf16[96,640]{1,0:T(8,128)(2,1)S(1)} %constant_dynamic-slice_fusion), channel_id=1, source_target_pairs={{0,1},{1,2},{2,3},{3,4},{4,5},{5,6},{6,7},{7,0},{8,9},{9,10},{10,1... | collective-permute-start | bytes 368648 | tf_op jit(solution)/shard_map/ppermute | solution.py:282
  10.7 3.0 %collective-permute-start.18 = (bf16[96,640]{1,0:T(8,128)(2,1)S(1)}, bf16[96,640]{1,0:T(8,128)(2,1)S(1)}, u32[]{:S(2)}, u32[]{:S(2)}) collective-permute-start(bf16[96,640]{1,0:T(8,128)(2,1)S(1)} %constant_dynamic-slice_fusion), channel_id=1, source_target_pairs={{0,2},{1,3},{2,4},{3,5},{4,6},{5,7},{6,0},{7,1},{8,10},{9,11},{10,... | collective-permute-start | bytes 368648 | tf_op jit(solution)/shard_map/ppermute | solution.py:282
  13.7 3.1 %collective-permute-start.17 = (bf16[96,640]{1,0:T(8,128)(2,1)S(1)}, bf16[96,640]{1,0:T(8,128)(2,1)S(1)}, u32[]{:S(2)}, u32[]{:S(2)}) collective-permute-start(bf16[96,640]{1,0:T(8,128)(2,1)S(1)} %constant_dynamic-slice_fusion), channel_id=1, source_target_pairs={{0,5},{1,6},{2,7},{3,0},{4,1},{5,2},{6,3},{7,4},{8,13},{9,14},{10,... | collective-permute-start | bytes 368648 | tf_op jit(solution)/shard_map/ppermute | solution.py:282
  16.8 3.0 %collective-permute-start.16 = (bf16[96,640]{1,0:T(8,128)(2,1)S(1)}, bf16[96,640]{1,0:T(8,128)(2,1)S(1)}, u32[]{:S(2)}, u32[]{:S(2)}) collective-permute-start(bf16[96,640]{1,0:T(8,128)(2,1)S(1)} %constant_dynamic-slice_fusion), channel_id=1, source_target_pairs={{0,6},{1,7},{2,0},{3,1},{4,2},{5,3},{6,4},{7,5},{8,14},{9,15},{10,... | collective-permute-start | bytes 368648 | tf_op jit(solution)/shard_map/ppermute | solution.py:282
  23.2 7.4 %shard_map.94 = (bf16[8,208,384]{2,1,0:T(8,128)(2,1)}, bf16[1536,384]{1,0:T(8,128)(2,1)S(1)}, bf16[128,128]{1,0:T(8,128)(2,1)}, s32[2]{0:T(128)}) custom-call(s32[2]{0:T(128)} %pad_add_fusion.place, s32[5,64]{1,0:T(8,128)} %bitcast.12, f32[8,128]{1,0:T(8,128)} %constant.28.clone.frequency, bf16[3,128,3072]{2,1,0:T(8,128)(2,1)} %rows.1, ...), custom_call_target="tpu_custom_call" | custom-call | flops 1000000000 | bytes 6000000 | tf_op jit(solution)/shard_map/pallas_call | solution.py:288
  30.6 3.3 %collective-permute-done.15 = bf16[96,640]{1,0:T(8,128)(2,1)S(1)} collective-permute-done((bf16[96,640]{1,0:T(8,128)(2,1)S(1)}, bf16[96,640]{1,0:T(8,128)(2,1)S(1)}, u32[]{:S(2)}, u32[]{:S(2)}) %collective-permute-start.15) | collective-permute-done | bytes 122912 | tf_op jit(solution)/shard_map/ppermute | solution.py:282
  34.0 39.4 %conditional.1 = (bf16[1536,384]{1,0:T(8,128)(2,1)}, bf16[8,208,384]{2,1,0:T(8,128)(2,1)}, bf16[96,640]{1,0:T(8,128)(2,1)}, bf16[96,640]{1,0:T(8,128)(2,1)}) conditional(s32[]{:T(128)} %clamp.3, (bf16[1536,384]{1,0:T(8,128)(2,1)S(1)}, bf16[8,208,384]{2,1,0:T(8,128)(2,1)}, bf16[96,640]{1,0:T(8,128)(2,1)S(1)}, ...), branch_computations={%region_1.0_spmd, %region_2.0_spmd, %region_3.0_spmd, %region_4.0_... | conditional | bytes 9535672 | solution.py:323
  34.0 5.1 %all-to-all-start.2 = ((bf16[8,208,384]{2,1,0:T(8,128)(2,1)}), bf16[8,208,384]{2,1,0:T(8,128)(2,1)}, u32[]{:S(2)}, u32[]{:S(2)}) async-start(bf16[8,208,384]{2,1,0:T(8,128)(2,1)} %get-tuple-element.49), calls=%async_computation.2 | async-start | bytes 2555904 | tf_op jit(solution)/shard_map/cond/branch_2_fun/all_to_all | solution.py:311
  39.1 2.7 %collective-permute-start.6 = (bf16[1536,384]{1,0:T(8,128)(2,1)S(1)}, bf16[1536,384]{1,0:T(8,128)(2,1)}, u32[]{:S(2)}, u32[]{:S(2)}) collective-permute-start(bf16[1536,384]{1,0:T(8,128)(2,1)S(1)} %get-tuple-element.48), channel_id=1, source_target_pairs={{0,32},{8,40},{16,48},{24,56},{32,0},{40,8},{48,16},{56,24},{64,96... | collective-permute-start | bytes 3538952 | tf_op jit(solution)/shard_map/cond/branch_2_fun/ppermute | solution.py:318
  41.9 2.7 %collective-permute-start.7 = (bf16[96,640]{1,0:T(8,128)(2,1)S(1)}, bf16[96,640]{1,0:T(8,128)(2,1)}, u32[]{:S(2)}, u32[]{:S(2)}) collective-permute-start(bf16[96,640]{1,0:T(8,128)(2,1)S(1)} %get-tuple-element.50), channel_id=1, source_target_pairs={{0,7},{1,0},{2,1},{3,2},{4,3},{5,4},{6,5},{7,6},{8,15},{9,8},{10,9... | collective-permute-start | bytes 368648 | tf_op jit(solution)/shard_map/cond/branch_2_fun/ppermute | solution.py:282
  44.6 25.5 %collective-permute-done.7 = bf16[96,640]{1,0:T(8,128)(2,1)} collective-permute-done((bf16[96,640]{1,0:T(8,128)(2,1)S(1)}, bf16[96,640]{1,0:T(8,128)(2,1)}, u32[]{:S(2)}, u32[]{:S(2)}) %collective-permute-start.7) | collective-permute-done | bytes 122912 | tf_op jit(solution)/shard_map/cond/branch_2_fun/ppermute | solution.py:282
  70.7 2.7 %all-to-all-done.2 = bf16[8,208,384]{2,1,0:T(8,128)(2,1)} async-done(((bf16[8,208,384]{2,1,0:T(8,128)(2,1)}), bf16[8,208,384]{2,1,0:T(8,128)(2,1)}, u32[]{:S(2)}, u32[]{:S(2)}) %all-to-all-start.2) | async-done | bytes 1277984 | tf_op jit(solution)/shard_map/cond/branch_2_fun/all_to_all | solution.py:311
  76.2 4.2 %all-to-all-start.5 = ((bf16[8,192,384]{2,1,0:T(8,128)(2,1)}), bf16[8,192,384]{2,1,0:T(8,128)(2,1)S(1)}, u32[]{:S(2)}, u32[]{:S(2)}) async-start(bf16[8,192,384]{2,1,0:T(8,128)(2,1)} %bitcast.3), calls=%async_computation.5 | async-start | bytes 2359296 | tf_op jit(solution)/shard_map/all_to_all | solution.py:311
  80.4 3.8 %shard_map.95.first = bf16[512,384]{1,0:T(8,128)(2,1)} custom-call(s32[2]{0:T(128)} %get-tuple-element.90.info, bf16[8,208,384]{2,1,0:T(8,128)(2,1)} %get-tuple-element.103.blocks.extras), custom_call_target="tpu_custom_call" | custom-call | flops 1000000000 | bytes 2000000 | tf_op jit(solution)/shard_map/pallas_call | solution.py:337
  84.2 28.3 %all-to-all-done.5.blocks = bf16[8,192,384]{2,1,0:T(8,128)(2,1)S(1)} async-done(((bf16[8,192,384]{2,1,0:T(8,128)(2,1)}), bf16[8,192,384]{2,1,0:T(8,128)(2,1)S(1)}, u32[]{:S(2)}, u32[]{:S(2)}) %all-to-all-start.5) | async-done | bytes 1179680 | tf_op jit(solution)/shard_map/all_to_all | solution.py:311
  113.5 4.5 %shard_map.96 = (bf16[8,128,384]{2,1,0:T(8,128)(2,1)}, f32[32,384]{1,0:T(8,128)}) custom-call(s32[2]{0:T(128)} %get-tuple-element.90.info, bf16[512,384]{1,0:T(8,128)(2,1)} %shard_map.95.first, bf16[8,208,384]{2,1,0:T(8,128)(2,1)} %get-tuple-element.103.blocks.extras, bf16[8,192,384]{2,1,0:T(8,128)(2,1)} %copy-done.1), custom_call_target="tpu_custom_call" | custom-call | flops 1000000000 | bytes 4000000 | tf_op jit(solution)/shard_map/pallas_call | solution.py:345
  117.9 27.5 %all_to_all.45.back = bf16[8,128,384]{2,1,0:T(8,128)(2,1)} all-to-all(bf16[8,128,384]{2,1,0:T(8,128)(2,1)} %get-tuple-element.105), channel_id=1, replica_groups=mesh['dp'=32,'seq'=8] {'seq'}, dimensions={0} | all-to-all | bytes 1572864 | tf_op jit(solution)/shard_map/all_to_all | solution.py:311
  145.5 3.8 %shard_map.97 = (bf16[128,3072]{1,0:T(8,128)(2,1)}, bf16[32,128]{1,0:T(8,128)(2,1)}, bf16[32,48,128]{2,1,0:T(8,128)(2,1)}) custom-call(bf16[8,128,384]{2,1,0:T(8,128)(2,1)} %all_to_all.45.back, bf16[128,128]{1,0:T(8,128)(2,1)} %get-tuple-element.106.to_rows, bf16[32,3072]{1,0:T(8,128)(2,1)} %bitcast.11, bf16[128,5120]{1,0:T(8,128)(2,1)} %cotangent.3, ...), custom_call_target="tpu_custom_call" | custom-call | flops 100000000 | bytes 2000000 | tf_op jit(solution)/shard_map/pallas_call | solution.py:357
  149.3 21.5 %all_to_all.46.parts = bf16[32,48,128]{2,1,0:T(8,128)(2,1)} all-to-all(bf16[32,48,128]{2,1,0:T(8,128)(2,1)} %get-tuple-element.110), channel_id=1, replica_groups=mesh['dp'=32,'seq'=8] {'dp'}, dimensions={0} | all-to-all | bytes 786432 | tf_op jit(solution)/shard_map/all_to_all | solution.py:311
  172.6 3.4 %all-to-all-start.8 = ((f32[8,48,128]{2,1,0:T(8,128)}), f32[8,48,128]{2,1,0:T(8,128)S(1)}, u32[]{:S(2)}, u32[]{:S(2)}) async-start(f32[8,48,128]{2,1,0:T(8,128)} %shard_map.98), calls=%async_computation.8 | async-start | bytes 393216 | tf_op jit(solution)/shard_map/all_to_all | solution.py:311
  176.0 4.2 %shard_map.100.refs_4_ = bf16[128,5120]{1,0:T(8,128)(2,1)} custom-call(s32[1]{0:T(128)} %bitcast.shard, bf16[128,3072]{1,0:T(8,128)(2,1)} %get-tuple-element.108.attended, bf16[32,128]{1,0:T(8,128)(2,1)} %get-tuple-element.109.adapted, bf16[32,5120]{1,0:T(8,128)(2,1)} %up.5, bf16[3072,640]{1,0:T(8,128)(2,1)} %own.1), custom_call_target="tpu_custom_call" | custom-call | flops 503316480 | bytes 3932160 | tf_op jit(solution)/shard_map/pallas_call | solution.py:382
  180.2 4.1 %all-to-all-done.8.parts = f32[8,48,128]{2,1,0:T(8,128)S(1)} async-done(((f32[8,48,128]{2,1,0:T(8,128)}), f32[8,48,128]{2,1,0:T(8,128)S(1)}, u32[]{:S(2)}, u32[]{:S(2)}) %all-to-all-start.8) | async-done | bytes 196640 | tf_op jit(solution)/shard_map/all_to_all | solution.py:311
  186.7 7.3 %all-to-all-start.9 = ((bf16[32,64,128]{2,1,0:T(8,128)(2,1)}), bf16[32,64,128]{2,1,0:T(8,128)(2,1)S(1)}, u32[]{:S(2)}, u32[]{:S(2)}) async-start(bf16[32,64,128]{2,1,0:T(8,128)(2,1)} %shard_map.99), calls=%async_computation.9 | async-start | bytes 1048576 | tf_op jit(solution)/shard_map/all_to_all | solution.py:311
  194.1 13.5 %shard_map.101 = bf16[128,5120]{1,0:T(8,128)(2,1)} custom-call(s32[1]{0:T(128)} %bitcast.shard, bf16[128,3072]{1,0:T(8,128)(2,1)} %get-tuple-element.108.attended, bf16[32,128]{1,0:T(8,128)(2,1)} %get-tuple-element.109.adapted, bf16[32,5120]{1,0:T(8,128)(2,1)} %up.5, bf16[32,7,96,640]{3,2,1,0:T(8,128)(2,1)} %bitcast.7, ...), custom_call_target="tpu_custom_call", output_to_operand_aliasing={{}: (8, {})} | custom-call | flops 4026531840 | bytes 31457280 | tf_op jit(solution)/shard_map/pallas_call | solution.py:421
  (33 shorter events, 15.7 us)
Async XLA Ops:
  7.2 179.6 %all-gather.2.cloned.1.call-start = ((), (), s32[]{:S(2)}) async-start(), calls=%async_computation.10 | async-start | bytes 28385280 | tf_op jit(solution)/shard_map/all_gather | solution.py:334
  8.1 22.5 %collective-permute-start.19 = (bf16[96,640]{1,0:T(8,128)(2,1)S(1)}, bf16[96,640]{1,0:T(8,128)(2,1)S(1)}, u32[]{:S(2)}, u32[]{:S(2)}) collective-permute-start(bf16[96,640]{1,0:T(8,128)(2,1)S(1)} %constant_dynamic-slice_fusion), channel_id=1, source_target_pairs={{0,1},{1,2},{2,3},{3,4},{4,5},{5,6},{6,7},{7,0},{8,9},{9,10},{10,1... | collective-permute-start | bytes 368648 | tf_op jit(solution)/shard_map/ppermute | solution.py:282
  10.7 19.9 %collective-permute-start.18 = (bf16[96,640]{1,0:T(8,128)(2,1)S(1)}, bf16[96,640]{1,0:T(8,128)(2,1)S(1)}, u32[]{:S(2)}, u32[]{:S(2)}) collective-permute-start(bf16[96,640]{1,0:T(8,128)(2,1)S(1)} %constant_dynamic-slice_fusion), channel_id=1, source_target_pairs={{0,2},{1,3},{2,4},{3,5},{4,6},{5,7},{6,0},{7,1},{8,10},{9,11},{10,... | collective-permute-start | bytes 368648 | tf_op jit(solution)/shard_map/ppermute | solution.py:282
  13.7 17.0 %collective-permute-start.17 = (bf16[96,640]{1,0:T(8,128)(2,1)S(1)}, bf16[96,640]{1,0:T(8,128)(2,1)S(1)}, u32[]{:S(2)}, u32[]{:S(2)}) collective-permute-start(bf16[96,640]{1,0:T(8,128)(2,1)S(1)} %constant_dynamic-slice_fusion), channel_id=1, source_target_pairs={{0,5},{1,6},{2,7},{3,0},{4,1},{5,2},{6,3},{7,4},{8,13},{9,14},{10,... | collective-permute-start | bytes 368648 | tf_op jit(solution)/shard_map/ppermute | solution.py:282
  16.8 13.8 %collective-permute-start.16 = (bf16[96,640]{1,0:T(8,128)(2,1)S(1)}, bf16[96,640]{1,0:T(8,128)(2,1)S(1)}, u32[]{:S(2)}, u32[]{:S(2)}) collective-permute-start(bf16[96,640]{1,0:T(8,128)(2,1)S(1)} %constant_dynamic-slice_fusion), channel_id=1, source_target_pairs={{0,6},{1,7},{2,0},{3,1},{4,2},{5,3},{6,4},{7,5},{8,14},{9,15},{10,... | collective-permute-start | bytes 368648 | tf_op jit(solution)/shard_map/ppermute | solution.py:282
  19.8 14.1 %collective-permute-start.15 = (bf16[96,640]{1,0:T(8,128)(2,1)S(1)}, bf16[96,640]{1,0:T(8,128)(2,1)S(1)}, u32[]{:S(2)}, u32[]{:S(2)}) collective-permute-start(bf16[96,640]{1,0:T(8,128)(2,1)S(1)} %constant_dynamic-slice_fusion), channel_id=1, source_target_pairs={{0,7},{1,0},{2,1},{3,2},{4,3},{5,4},{6,5},{7,6},{8,15},{9,8},{10,9... | collective-permute-start | bytes 368648 | tf_op jit(solution)/shard_map/ppermute | solution.py:282
  34.0 39.3 %all-to-all-start.2 = ((bf16[8,208,384]{2,1,0:T(8,128)(2,1)}), bf16[8,208,384]{2,1,0:T(8,128)(2,1)}, u32[]{:S(2)}, u32[]{:S(2)}) async-start(bf16[8,208,384]{2,1,0:T(8,128)(2,1)} %get-tuple-element.49), calls=%async_computation.2 | async-start | bytes 2555904 | tf_op jit(solution)/shard_map/cond/branch_2_fun/all_to_all | solution.py:311
  39.1 31.6 %collective-permute-start.6 = (bf16[1536,384]{1,0:T(8,128)(2,1)S(1)}, bf16[1536,384]{1,0:T(8,128)(2,1)}, u32[]{:S(2)}, u32[]{:S(2)}) collective-permute-start(bf16[1536,384]{1,0:T(8,128)(2,1)S(1)} %get-tuple-element.48), channel_id=1, source_target_pairs={{0,32},{8,40},{16,48},{24,56},{32,0},{40,8},{48,16},{56,24},{64,96... | collective-permute-start | bytes 3538952 | tf_op jit(solution)/shard_map/cond/branch_2_fun/ppermute | solution.py:318
  41.9 28.2 %collective-permute-start.7 = (bf16[96,640]{1,0:T(8,128)(2,1)S(1)}, bf16[96,640]{1,0:T(8,128)(2,1)}, u32[]{:S(2)}, u32[]{:S(2)}) collective-permute-start(bf16[96,640]{1,0:T(8,128)(2,1)S(1)} %get-tuple-element.50), channel_id=1, source_target_pairs={{0,7},{1,0},{2,1},{3,2},{4,3},{5,4},{6,5},{7,6},{8,15},{9,8},{10,9... | collective-permute-start | bytes 368648 | tf_op jit(solution)/shard_map/cond/branch_2_fun/ppermute | solution.py:282
  44.6 26.2 %collective-permute-start.8 = (bf16[96,640]{1,0:T(8,128)(2,1)S(1)}, bf16[96,640]{1,0:T(8,128)(2,1)}, u32[]{:S(2)}, u32[]{:S(2)}) collective-permute-start(bf16[96,640]{1,0:T(8,128)(2,1)S(1)} %get-tuple-element.51), channel_id=1, source_target_pairs={{0,1},{1,2},{2,3},{3,4},{4,5},{5,6},{6,7},{7,0},{8,9},{9,10},{10,1... | collective-permute-start | bytes 368648 | tf_op jit(solution)/shard_map/cond/branch_2_fun/ppermute | solution.py:282
  75.3 0.9 copy-start.2
  76.2 36.3 %all-to-all-start.5 = ((bf16[8,192,384]{2,1,0:T(8,128)(2,1)}), bf16[8,192,384]{2,1,0:T(8,128)(2,1)S(1)}, u32[]{:S(2)}, u32[]{:S(2)}) async-start(bf16[8,192,384]{2,1,0:T(8,128)(2,1)} %bitcast.3), calls=%async_computation.5 | async-start | bytes 2359296 | tf_op jit(solution)/shard_map/all_to_all | solution.py:311
  112.5 1.0 copy-start.1
  172.6 11.7 %all-to-all-start.8 = ((f32[8,48,128]{2,1,0:T(8,128)}), f32[8,48,128]{2,1,0:T(8,128)S(1)}, u32[]{:S(2)}, u32[]{:S(2)}) async-start(f32[8,48,128]{2,1,0:T(8,128)} %shard_map.98), calls=%async_computation.8 | async-start | bytes 393216 | tf_op jit(solution)/shard_map/all_to_all | solution.py:311
  184.3 0.7 copy-start.3
  186.7 20.8 %all-to-all-start.9 = ((bf16[32,64,128]{2,1,0:T(8,128)(2,1)}), bf16[32,64,128]{2,1,0:T(8,128)(2,1)S(1)}, u32[]{:S(2)}, u32[]{:S(2)}) async-start(bf16[32,64,128]{2,1,0:T(8,128)(2,1)} %shard_map.99), calls=%async_computation.9 | async-start | bytes 1048576 | tf_op jit(solution)/shard_map/all_to_all | solution.py:311
  207.6 0.8 copy-start
Sparse Core Ops, SparseCore 0:
  76.3 106.9 all-gather.1

commit v3 on v2

--- a/solution.py
+++ b/solution.py
@@ -12,8 +12,7 @@
 HEAD = 128
 SLOT = 64
 ADAPTER_SCALE = 2.0
-FAR = (4, 5)
-GATHERED = (1, 2, 3, 6, 7, 4, 5)
+FAR = (3, 4, 5)
 STREAMS = 4
 VMEM_BYTES = 56 * 1024 * 1024
 F32 = jnp.float32
@@ -314,22 +313,22 @@
     bits = dp_count.bit_length() - 1
     branch = jnp.max(sum((apart > (1 << b)).astype(jnp.int32) for b in range(bits - 1)))
 
-    def move(bit, moving, stay, above, below):
+    def move(bit, moving, stay, pair, below):
         moved = lax.ppermute(moving, "dp", [(g, g ^ (1 << bit)) for g in range(dp_count)])
-        return moved, exchange(stay, "seq"), turn(above, -1), turn(below, 1)
-
-    moving, *blocks = lax.optimization_barrier((moving, *near.values()))
+        return moved, exchange(stay, "seq"), turn(pair, -2), turn(below, 1)
+
+    pair = jnp.concatenate([near[1], near[2]], axis=0)
+    moving, pair, *blocks = lax.optimization_barrier((moving, pair, *near.values()))
     blocks = dict(zip(near, blocks))
     moved, stay, *far = lax.switch(
         branch,
         [functools.partial(move, bit) for bit in range(bits)],
         moving,
         stay,
-        blocks[FAR[0] - 1],
-        blocks[FAR[1] + 1],
-    )
-    blocks |= dict(zip(FAR, far))
-    others = jnp.concatenate([blocks[k] for k in GATHERED], axis=0)
+        pair,
+        blocks[6],
+    )
+    others = jnp.concatenate([pair, blocks[6], blocks[7], *far], axis=0)
     others, moved, stay = lax.optimization_barrier((others, moved, stay))
     gathered = lax.all_gather(others, "dp", axis=0, tiled=True)
     gathered = gathered.reshape(dp_count, seq_count - 1, weight_rows, feature_dev)
@@ -376,7 +375,7 @@
         return (0, s[0])
 
     def gathered_block(k, s):
-        away = jnp.where(k < 3, k + 1, jnp.where(k < 5, k + 3, k - 1))
+        away = jnp.where(k < 2, k + 1, jnp.where(k < 4, k + 4, k - 1))
         return (0, lax.rem(s[0] + away, 8))
 
     begun = pl.pallas_call(

time: 219 us -> 218 us (level)
  waiting for transfers between devices: 64.5 us -> 59.7 us
  starting transfers between devices: 37.9 us -> 42.3 us
    all_to_all x4, starting transfers between devices: 20 us -> 26.8 us  [exchange(): return lax.all_to_all(block, axis, split_axis=0, concat_axis=0, tiled=True)]
    ppermute x7 -> x6, waiting for transfers between devices: 29.5 us -> 24.3 us  [turn(): lax.ppermute(block, 'seq', [(i, (i + k) % seq_count) for i in range(seq_c...]
    ppermute x7 -> x6, starting transfers between devices: 15.1 us -> 12.8 us  [turn(): lax.ppermute(block, 'seq', [(i, (i + k) % seq_count) for i in range(seq_c...]
    unnamed x14 -> x12, local copies, waits for them, and re-layouts: 4.41 us -> 4.43 us
  transfers between devices with their start and end apart: 13 -> 12, of which waited for: 6 -> 5; matrix products, arithmetic and copies ran while one was open for 1% -> 1% of each run, Pallas kernels for 19% -> 19%
where the time goes in v3:
time: 218 us; the launch traced here: 217 us
  waiting for transfers between devices  59.7 us (27%)
  blocking collectives  49 us (22%)
  Pallas kernels  43 us (20%)
  starting transfers between devices  42.3 us (19%)
  between operations  14.8 us (7%)
  local copies, waits for them, and re-layouts  6.27 us (3%)
    all_to_all x2, blocking collectives, exchange(): return lax.all_to_all(block, axis, split_axis=0, concat_axis=0, tiled=True)  49 us
    all_to_all x4, waiting for transfers between devices, exchange(): return lax.all_to_all(block, axis, split_axis=0, concat_axis=0, tiled=True)  35.4 us
    all_to_all x4, starting transfers between devices, exchange(): return lax.all_to_all(block, axis, split_axis=0, concat_axis=0, tiled=True)  26.8 us
    ppermute x6, waiting for transfers between devices, turn(): lax.ppermute(block, 'seq', [(i, (i + k) % seq_count) for i in range(seq_c...  24.3 us
    pallas_call x1, Pallas kernels, body(): pl.pallas_call(project, grid_spec=pltpu.PrefetchScalarGridSpec(num_scalar...  13.5 us
    ppermute x6, starting transfers between devices, turn(): lax.ppermute(block, 'seq', [(i, (i + k) % seq_count) for i in range(seq_c...  12.8 us
    pallas_call x1, Pallas kernels, body(): call(prepare, [SM, SM, VM, VM, VM, VM], [struct((seq_count, 3 * SLOT + ra...  7.39 us
    pallas_call x1, Pallas kernels, body(): call(attend_second, [SM] + [VM] * 3, [struct((seq_count, 2 * SLOT, width_...  4.47 us
  transfers between devices with their start and end apart: 12, of which 5 were waited for; matrix products, arithmetic and copies ran while one was open for 1% of the time, Pallas kernels for 19%

profile of v3, /device:TPU:1, one launch (start us, length us, event | category | flops | bytes accessed | tf_op | source)
XLA Modules:
  0.0 217.3 jit_solution(1893487832610888867)
XLA Ops:
  8.1 2.5 %collective-permute-start.18 = (bf16[96,640]{1,0:T(8,128)(2,1)S(1)}, bf16[96,640]{1,0:T(8,128)(2,1)S(1)}, u32[]{:S(2)}, u32[]{:S(2)}) collective-permute-start(bf16[96,640]{1,0:T(8,128)(2,1)S(1)} %constant_dynamic-slice_fusion), channel_id=1, source_target_pairs={{0,1},{1,2},{2,3},{3,4},{4,5},{5,6},{6,7},{7,0},{8,9},{9,10},{10,1... | collective-permute-start | bytes 368648 | tf_op jit(solution)/shard_map/ppermute | solution.py:281
  10.7 3.0 %collective-permute-start.17 = (bf16[96,640]{1,0:T(8,128)(2,1)S(1)}, bf16[96,640]{1,0:T(8,128)(2,1)S(1)}, u32[]{:S(2)}, u32[]{:S(2)}) collective-permute-start(bf16[96,640]{1,0:T(8,128)(2,1)S(1)} %constant_dynamic-slice_fusion), channel_id=1, source_target_pairs={{0,2},{1,3},{2,4},{3,5},{4,6},{5,7},{6,0},{7,1},{8,10},{9,11},{10,... | collective-permute-start | bytes 368648 | tf_op jit(solution)/shard_map/ppermute | solution.py:281
  13.7 2.1 collective-permute-start.16
  19.1 7.4 %shard_map.94 = (bf16[8,208,384]{2,1,0:T(8,128)(2,1)}, bf16[1536,384]{1,0:T(8,128)(2,1)S(1)}, bf16[128,128]{1,0:T(8,128)(2,1)}, s32[2]{0:T(128)}) custom-call(s32[2]{0:T(128)} %pad_add_fusion.place, s32[5,64]{1,0:T(8,128)} %bitcast.12, f32[8,128]{1,0:T(8,128)} %constant.28.clone.frequency, bf16[3,128,3072]{2,1,0:T(8,128)(2,1)} %rows.1, ...), custom_call_target="tpu_custom_call" | custom-call | flops 1000000000 | bytes 6000000 | tf_op jit(solution)/shard_map/pallas_call | solution.py:287
  27.3 39.0 %conditional.1 = (bf16[1536,384]{1,0:T(8,128)(2,1)}, bf16[8,208,384]{2,1,0:T(8,128)(2,1)}, bf16[192,640]{1,0:T(8,128)(2,1)}, bf16[96,640]{1,0:T(8,128)(2,1)}) conditional(s32[]{:T(128)} %clamp.3, (bf16[1536,384]{1,0:T(8,128)(2,1)S(1)}, bf16[8,208,384]{2,1,0:T(8,128)(2,1)}, bf16[192,640]{1,0:T(8,128)(2,1)S(1)}, ...), branch_computations={%region_1.0_spmd, %region_2.0_spmd, %region_3.0_spmd, %region_4.0_... | conditional | bytes 10027192 | solution.py:323
  27.4 5.2 %all-to-all-start.2 = ((bf16[8,208,384]{2,1,0:T(8,128)(2,1)}), bf16[8,208,384]{2,1,0:T(8,128)(2,1)}, u32[]{:S(2)}, u32[]{:S(2)}) async-start(bf16[8,208,384]{2,1,0:T(8,128)(2,1)} %get-tuple-element.49), calls=%async_computation.2 | async-start | bytes 2555904 | tf_op jit(solution)/shard_map/cond/branch_2_fun/all_to_all | solution.py:310
  32.6 2.7 %collective-permute-start.6 = (bf16[1536,384]{1,0:T(8,128)(2,1)S(1)}, bf16[1536,384]{1,0:T(8,128)(2,1)}, u32[]{:S(2)}, u32[]{:S(2)}) collective-permute-start(bf16[1536,384]{1,0:T(8,128)(2,1)S(1)} %get-tuple-element.48), channel_id=1, source_target_pairs={{0,32},{8,40},{16,48},{24,56},{32,0},{40,8},{48,16},{56,24},{64,96... | collective-permute-start | bytes 3538952 | tf_op jit(solution)/shard_map/cond/branch_2_fun/ppermute | solution.py:317
  35.3 3.6 %collective-permute-start.7 = (bf16[192,640]{1,0:T(8,128)(2,1)S(1)}, bf16[192,640]{1,0:T(8,128)(2,1)}, u32[]{:S(2)}, u32[]{:S(2)}) collective-permute-start(bf16[192,640]{1,0:T(8,128)(2,1)S(1)} %get-tuple-element.50), channel_id=1, source_target_pairs={{0,6},{1,7},{2,0},{3,1},{4,2},{5,3},{6,4},{7,5},{8,14},{9,15},{10,... | collective-permute-start | bytes 737288 | tf_op jit(solution)/shard_map/cond/branch_2_fun/ppermute | solution.py:281
  39.2 23.8 %collective-permute-done.8 = bf16[96,640]{1,0:T(8,128)(2,1)} collective-permute-done((bf16[96,640]{1,0:T(8,128)(2,1)S(1)}, bf16[96,640]{1,0:T(8,128)(2,1)}, u32[]{:S(2)}, u32[]{:S(2)}) %collective-permute-start.8) | collective-permute-done | bytes 122912 | tf_op jit(solution)/shard_map/cond/branch_2_fun/ppermute | solution.py:281
  63.4 2.9 %all-to-all-done.2 = bf16[8,208,384]{2,1,0:T(8,128)(2,1)} async-done(((bf16[8,208,384]{2,1,0:T(8,128)(2,1)}), bf16[8,208,384]{2,1,0:T(8,128)(2,1)}, u32[]{:S(2)}, u32[]{:S(2)}) %all-to-all-start.2) | async-done | bytes 1277984 | tf_op jit(solution)/shard_map/cond/branch_2_fun/all_to_all | solution.py:310
  69.2 10.8 %all-to-all-start.5 = ((bf16[8,192,384]{2,1,0:T(8,128)(2,1)}), bf16[8,192,384]{2,1,0:T(8,128)(2,1)S(1)}, u32[]{:S(2)}, u32[]{:S(2)}) async-start(bf16[8,192,384]{2,1,0:T(8,128)(2,1)} %bitcast.3), calls=%async_computation.5 | async-start | bytes 2359296 | tf_op jit(solution)/shard_map/all_to_all | solution.py:310
  80.0 3.8 %shard_map.95.first = bf16[512,384]{1,0:T(8,128)(2,1)} custom-call(s32[2]{0:T(128)} %get-tuple-element.88.info, bf16[8,208,384]{2,1,0:T(8,128)(2,1)} %get-tuple-element.99.blocks.extras), custom_call_target="tpu_custom_call" | custom-call | flops 1000000000 | bytes 2000000 | tf_op jit(solution)/shard_map/pallas_call | solution.py:336
  83.7 28.2 %all-to-all-done.5.blocks = bf16[8,192,384]{2,1,0:T(8,128)(2,1)S(1)} async-done(((bf16[8,192,384]{2,1,0:T(8,128)(2,1)}), bf16[8,192,384]{2,1,0:T(8,128)(2,1)S(1)}, u32[]{:S(2)}, u32[]{:S(2)}) %all-to-all-start.5) | async-done | bytes 1179680 | tf_op jit(solution)/shard_map/all_to_all | solution.py:310
  113.0 4.5 %shard_map.96 = (bf16[8,128,384]{2,1,0:T(8,128)(2,1)}, f32[32,384]{1,0:T(8,128)}) custom-call(s32[2]{0:T(128)} %get-tuple-element.88.info, bf16[512,384]{1,0:T(8,128)(2,1)} %shard_map.95.first, bf16[8,208,384]{2,1,0:T(8,128)(2,1)} %get-tuple-element.99.blocks.extras, bf16[8,192,384]{2,1,0:T(8,128)(2,1)} %copy-done.2), custom_call_target="tpu_custom_call" | custom-call | flops 1000000000 | bytes 4000000 | tf_op jit(solution)/shard_map/pallas_call | solution.py:344
  117.4 27.2 %all_to_all.45.back = bf16[8,128,384]{2,1,0:T(8,128)(2,1)} all-to-all(bf16[8,128,384]{2,1,0:T(8,128)(2,1)} %get-tuple-element.101), channel_id=1, replica_groups=mesh['dp'=32,'seq'=8] {'seq'}, dimensions={0} | all-to-all | bytes 1572864 | tf_op jit(solution)/shard_map/all_to_all | solution.py:310
  144.7 4.0 %shard_map.97 = (bf16[128,3072]{1,0:T(8,128)(2,1)}, bf16[32,128]{1,0:T(8,128)(2,1)}, bf16[32,48,128]{2,1,0:T(8,128)(2,1)}) custom-call(bf16[8,128,384]{2,1,0:T(8,128)(2,1)} %all_to_all.45.back, bf16[128,128]{1,0:T(8,128)(2,1)} %get-tuple-element.102.to_rows, bf16[32,3072]{1,0:T(8,128)(2,1)} %bitcast.11, bf16[128,5120]{1,0:T(8,128)(2,1)} %cotangent.3, ...), custom_call_target="tpu_custom_call" | custom-call | flops 100000000 | bytes 2000000 | tf_op jit(solution)/shard_map/pallas_call | solution.py:356
  148.6 21.8 %all_to_all.46.parts = bf16[32,48,128]{2,1,0:T(8,128)(2,1)} all-to-all(bf16[32,48,128]{2,1,0:T(8,128)(2,1)} %get-tuple-element.106), channel_id=1, replica_groups=mesh['dp'=32,'seq'=8] {'dp'}, dimensions={0} | all-to-all | bytes 786432 | tf_op jit(solution)/shard_map/all_to_all | solution.py:310
  172.2 3.4 %all-to-all-start.8 = ((f32[8,48,128]{2,1,0:T(8,128)}), f32[8,48,128]{2,1,0:T(8,128)S(1)}, u32[]{:S(2)}, u32[]{:S(2)}) async-start(f32[8,48,128]{2,1,0:T(8,128)} %shard_map.98), calls=%async_computation.8 | async-start | bytes 393216 | tf_op jit(solution)/shard_map/all_to_all | solution.py:310
  175.6 4.0 %shard_map.100.refs_4_ = bf16[128,5120]{1,0:T(8,128)(2,1)} custom-call(s32[1]{0:T(128)} %bitcast.shard, bf16[128,3072]{1,0:T(8,128)(2,1)} %get-tuple-element.104.attended, bf16[32,128]{1,0:T(8,128)(2,1)} %get-tuple-element.105.adapted, bf16[32,5120]{1,0:T(8,128)(2,1)} %up.5, bf16[3072,640]{1,0:T(8,128)(2,1)} %own.1), custom_call_target="tpu_custom_call" | custom-call | flops 503316480 | bytes 3932160 | tf_op jit(solution)/shard_map/pallas_call | solution.py:381
  179.5 4.3 %all-to-all-done.8.parts = f32[8,48,128]{2,1,0:T(8,128)S(1)} async-done(((f32[8,48,128]{2,1,0:T(8,128)}), f32[8,48,128]{2,1,0:T(8,128)S(1)}, u32[]{:S(2)}, u32[]{:S(2)}) %all-to-all-start.8) | async-done | bytes 196640 | tf_op jit(solution)/shard_map/all_to_all | solution.py:310
  184.5 1.8 shard_map.99
  186.3 7.4 %all-to-all-start.9 = ((bf16[32,64,128]{2,1,0:T(8,128)(2,1)}), bf16[32,64,128]{2,1,0:T(8,128)(2,1)S(1)}, u32[]{:S(2)}, u32[]{:S(2)}) async-start(bf16[32,64,128]{2,1,0:T(8,128)(2,1)} %shard_map.99), calls=%async_computation.9 | async-start | bytes 1048576 | tf_op jit(solution)/shard_map/all_to_all | solution.py:310
  193.7 13.5 %shard_map.101 = bf16[128,5120]{1,0:T(8,128)(2,1)} custom-call(s32[1]{0:T(128)} %bitcast.shard, bf16[128,3072]{1,0:T(8,128)(2,1)} %get-tuple-element.104.attended, bf16[32,128]{1,0:T(8,128)(2,1)} %get-tuple-element.105.adapted, bf16[32,5120]{1,0:T(8,128)(2,1)} %up.5, bf16[32,7,96,640]{3,2,1,0:T(8,128)(2,1)} %bitcast.7, ...), custom_call_target="tpu_custom_call", output_to_operand_aliasing={{}: (8, {})} | custom-call | flops 4026531840 | bytes 31457280 | tf_op jit(solution)/shard_map/pallas_call | solution.py:420
  208.0 2.5 %shard_map.102 = (f32[32,5120]{1,0:T(8,128)}, f32[32,3072]{1,0:T(8,128)}) custom-call(bf16[32,64,128]{2,1,0:T(8,128)(2,1)} %copy-done), custom_call_target="tpu_custom_call" | custom-call | tf_op jit(solution)/shard_map/pallas_call | solution.py:413
  (30 shorter events, 12.1 us)
Async XLA Ops:
  7.2 179.2 %all-gather.2.cloned.1.call-start = ((), (), s32[]{:S(2)}) async-start(), calls=%async_computation.10 | async-start | bytes 28385280 | tf_op jit(solution)/shard_map/all_gather | solution.py:333
  8.1 19.1 %collective-permute-start.18 = (bf16[96,640]{1,0:T(8,128)(2,1)S(1)}, bf16[96,640]{1,0:T(8,128)(2,1)S(1)}, u32[]{:S(2)}, u32[]{:S(2)}) collective-permute-start(bf16[96,640]{1,0:T(8,128)(2,1)S(1)} %constant_dynamic-slice_fusion), channel_id=1, source_target_pairs={{0,1},{1,2},{2,3},{3,4},{4,5},{5,6},{6,7},{7,0},{8,9},{9,10},{10,1... | collective-permute-start | bytes 368648 | tf_op jit(solution)/shard_map/ppermute | solution.py:281
  10.7 16.6 %collective-permute-start.17 = (bf16[96,640]{1,0:T(8,128)(2,1)S(1)}, bf16[96,640]{1,0:T(8,128)(2,1)S(1)}, u32[]{:S(2)}, u32[]{:S(2)}) collective-permute-start(bf16[96,640]{1,0:T(8,128)(2,1)S(1)} %constant_dynamic-slice_fusion), channel_id=1, source_target_pairs={{0,2},{1,3},{2,4},{3,5},{4,6},{5,7},{6,0},{7,1},{8,10},{9,11},{10,... | collective-permute-start | bytes 368648 | tf_op jit(solution)/shard_map/ppermute | solution.py:281
  13.7 13.5 %collective-permute-start.16 = (bf16[96,640]{1,0:T(8,128)(2,1)S(1)}, bf16[96,640]{1,0:T(8,128)(2,1)S(1)}, u32[]{:S(2)}, u32[]{:S(2)}) collective-permute-start(bf16[96,640]{1,0:T(8,128)(2,1)S(1)} %constant_dynamic-slice_fusion), channel_id=1, source_target_pairs={{0,6},{1,7},{2,0},{3,1},{4,2},{5,3},{6,4},{7,5},{8,14},{9,15},{10,... | collective-permute-start | bytes 368648 | tf_op jit(solution)/shard_map/ppermute | solution.py:281
  15.8 11.4 %collective-permute-start.15 = (bf16[96,640]{1,0:T(8,128)(2,1)S(1)}, bf16[96,640]{1,0:T(8,128)(2,1)S(1)}, u32[]{:S(2)}, u32[]{:S(2)}) collective-permute-start(bf16[96,640]{1,0:T(8,128)(2,1)S(1)} %constant_dynamic-slice_fusion), channel_id=1, source_target_pairs={{0,7},{1,0},{2,1},{3,2},{4,3},{5,4},{6,5},{7,6},{8,15},{9,8},{10,9... | collective-permute-start | bytes 368648 | tf_op jit(solution)/shard_map/ppermute | solution.py:281
  27.4 39.0 %all-to-all-start.2 = ((bf16[8,208,384]{2,1,0:T(8,128)(2,1)}), bf16[8,208,384]{2,1,0:T(8,128)(2,1)}, u32[]{:S(2)}, u32[]{:S(2)}) async-start(bf16[8,208,384]{2,1,0:T(8,128)(2,1)} %get-tuple-element.49), calls=%async_computation.2 | async-start | bytes 2555904 | tf_op jit(solution)/shard_map/cond/branch_2_fun/all_to_all | solution.py:310
  32.6 30.9 %collective-permute-start.6 = (bf16[1536,384]{1,0:T(8,128)(2,1)S(1)}, bf16[1536,384]{1,0:T(8,128)(2,1)}, u32[]{:S(2)}, u32[]{:S(2)}) collective-permute-start(bf16[1536,384]{1,0:T(8,128)(2,1)S(1)} %get-tuple-element.48), channel_id=1, source_target_pairs={{0,32},{8,40},{16,48},{24,56},{32,0},{40,8},{48,16},{56,24},{64,96... | collective-permute-start | bytes 3538952 | tf_op jit(solution)/shard_map/cond/branch_2_fun/ppermute | solution.py:317
  35.3 28.1 %collective-permute-start.7 = (bf16[192,640]{1,0:T(8,128)(2,1)S(1)}, bf16[192,640]{1,0:T(8,128)(2,1)}, u32[]{:S(2)}, u32[]{:S(2)}) collective-permute-start(bf16[192,640]{1,0:T(8,128)(2,1)S(1)} %get-tuple-element.50), channel_id=1, source_target_pairs={{0,6},{1,7},{2,0},{3,1},{4,2},{5,3},{6,4},{7,5},{8,14},{9,15},{10,... | collective-permute-start | bytes 737288 | tf_op jit(solution)/shard_map/cond/branch_2_fun/ppermute | solution.py:281
  38.9 24.1 %collective-permute-start.8 = (bf16[96,640]{1,0:T(8,128)(2,1)S(1)}, bf16[96,640]{1,0:T(8,128)(2,1)}, u32[]{:S(2)}, u32[]{:S(2)}) collective-permute-start(bf16[96,640]{1,0:T(8,128)(2,1)S(1)} %get-tuple-element.51), channel_id=1, source_target_pairs={{0,1},{1,2},{2,3},{3,4},{4,5},{5,6},{6,7},{7,0},{8,9},{9,10},{10,1... | collective-permute-start | bytes 368648 | tf_op jit(solution)/shard_map/cond/branch_2_fun/ppermute | solution.py:281
  68.3 0.9 copy-start.1
  69.2 42.7 %all-to-all-start.5 = ((bf16[8,192,384]{2,1,0:T(8,128)(2,1)}), bf16[8,192,384]{2,1,0:T(8,128)(2,1)S(1)}, u32[]{:S(2)}, u32[]{:S(2)}) async-start(bf16[8,192,384]{2,1,0:T(8,128)(2,1)} %bitcast.3), calls=%async_computation.5 | async-start | bytes 2359296 | tf_op jit(solution)/shard_map/all_to_all | solution.py:310
  111.9 1.0 copy-start.2
  172.2 11.7 %all-to-all-start.8 = ((f32[8,48,128]{2,1,0:T(8,128)}), f32[8,48,128]{2,1,0:T(8,128)S(1)}, u32[]{:S(2)}, u32[]{:S(2)}) async-start(f32[8,48,128]{2,1,0:T(8,128)} %shard_map.98), calls=%async_computation.8 | async-start | bytes 393216 | tf_op jit(solution)/shard_map/all_to_all | solution.py:310
  183.9 0.7 copy-start.3
  186.3 20.9 %all-to-all-start.9 = ((bf16[32,64,128]{2,1,0:T(8,128)(2,1)}), bf16[32,64,128]{2,1,0:T(8,128)(2,1)S(1)}, u32[]{:S(2)}, u32[]{:S(2)}) async-start(bf16[32,64,128]{2,1,0:T(8,128)(2,1)} %shard_map.99), calls=%async_computation.9 | async-start | bytes 1048576 | tf_op jit(solution)/shard_map/all_to_all | solution.py:310
  207.2 0.8 copy-start
Sparse Core Ops, SparseCore 0:
  69.3 114.9 all-gather.1

commit v4 on v3

--- a/solution.py
+++ b/solution.py
@@ -70,8 +70,14 @@
     return jnp.where((row == token + offset) & (token < portion), 1.0, 0.0).astype(BF16)
 
 
-def prepare(place, table, frequency, rows, cotangent, up, *outs):
-    stay_out, move_out, to_rows, info = outs
+def prepare(
+    place, table, frequency, rows_far, cotangent_far, up, stay_out, move_out, to_rows, info,
+    rows, cotangent, arrived,
+):
+    cotangent_copy = pltpu.make_async_copy(cotangent_far, cotangent, arrived.at[0])
+    rows_copy = pltpu.make_async_copy(rows_far, rows, arrived.at[1])
+    cotangent_copy.start()
+    rows_copy.start()
     group, shard = place[0], place[1]
     stay, leave, arrive = my_clips(table, group)
     zero = jnp.int32(0)
@@ -112,9 +118,11 @@
     even = lane % 2 == 0
     sine_next, sine_last = jnp.where(even, -sine, 0.0), jnp.where(even, 0.0, sine)
 
+    cotangent_copy.wait()
     low = (ADAPTER_SCALE * contract(up[...], cotangent[...], 1, 1)).astype(BF16)
     low = contract(low, target_rows, 1, 0).astype(BF16)
     half = low.shape[0] // 2
+    rows_copy.wait()
 
     width_dev = stay_out.shape[2]
     for k in range(8):
@@ -252,6 +260,7 @@
 
 VM = pl.BlockSpec(memory_space=pltpu.VMEM)
 SM = pl.BlockSpec(memory_space=pltpu.SMEM)
+FAR_AWAY = pl.BlockSpec(memory_space=pl.ANY)
 
 
 def call(kernel, in_specs, out_shapes, out_specs=None, flops=0, size=0, scratch=()):
@@ -286,7 +295,7 @@
 
     prepared = call(
         prepare,
-        [SM, SM, VM, VM, VM, VM],
+        [SM, SM, VM, FAR_AWAY, FAR_AWAY, VM],
         [
             struct((seq_count, 3 * SLOT + rank // 2, width_dev), BF16),
             struct((seq_count * 3 * SLOT, width_dev), BF16),
@@ -294,6 +303,11 @@
             struct((2,), jnp.int32),
         ],
         [VM] * 3 + [SM],
+        scratch=[
+            pltpu.VMEM(attention_inputs.shape, BF16),
+            pltpu.VMEM(cotangent.shape, BF16),
+            pltpu.SemaphoreType.DMA((2,)),
+        ],
         flops=10**9,
         size=6 * 10**6,
     )(

time: 218 us -> 218 us (level)
  transfers between devices with their start and end apart: 12 -> 12, of which waited for: 5 -> 5; matrix products, arithmetic and copies ran while one was open for 1% -> 1% of each run, Pallas kernels for 19% -> 18%
where the time goes in v4:
time: 218 us; the launch traced here: 217 us
  waiting for transfers between devices  60.1 us (28%)
  blocking collectives  49 us (22%)
  Pallas kernels  42.3 us (19%)
  starting transfers between devices  41.9 us (19%)
  between operations  14.8 us (7%)
  local copies, waits for them, and re-layouts  6.27 us (3%)
    all_to_all x2, blocking collectives, exchange(): return lax.all_to_all(block, axis, split_axis=0, concat_axis=0, tiled=True)  49 us
    all_to_all x4, waiting for transfers between devices, exchange(): return lax.all_to_all(block, axis, split_axis=0, concat_axis=0, tiled=True)  35.4 us
    all_to_all x4, starting transfers between devices, exchange(): return lax.all_to_all(block, axis, split_axis=0, concat_axis=0, tiled=True)  26.7 us
    ppermute x6, waiting for transfers between devices, turn(): lax.ppermute(block, 'seq', [(i, (i + k) % seq_count) for i in range(seq_c...  24.7 us
    pallas_call x1, Pallas kernels, body(): pl.pallas_call(project, grid_spec=pltpu.PrefetchScalarGridSpec(num_scalar...  13.5 us
    ppermute x6, starting transfers between devices, turn(): lax.ppermute(block, 'seq', [(i, (i + k) % seq_count) for i in range(seq_c...  13.1 us
    pallas_call x1, Pallas kernels, body(): call(prepare, [SM, SM, VM, FAR_AWAY, FAR_AWAY, VM], [struct((seq_count, 3...  6.76 us
    pallas_call x1, Pallas kernels, body(): call(attend_second, [SM] + [VM] * 3, [struct((seq_count, 2 * SLOT, width_...  4.47 us
  transfers between devices with their start and end apart: 12, of which 5 were waited for; matrix products, arithmetic and copies ran while one was open for 1% of the time, Pallas kernels for 18%

profile of v4, /device:TPU:1, one launch (start us, length us, event | category | flops | bytes accessed | tf_op | source)
XLA Modules:
  0.0 216.6 jit_solution(17080362116977895841)
XLA Ops:
  8.1 2.5 %collective-permute-start.18 = (bf16[96,640]{1,0:T(8,128)(2,1)S(1)}, bf16[96,640]{1,0:T(8,128)(2,1)S(1)}, u32[]{:S(2)}, u32[]{:S(2)}) collective-permute-start(bf16[96,640]{1,0:T(8,128)(2,1)S(1)} %constant_dynamic-slice_fusion), channel_id=1, source_target_pairs={{0,1},{1,2},{2,3},{3,4},{4,5},{5,6},{6,7},{7,0},{8,9},{9,10},{10,1... | collective-permute-start | bytes 368648 | tf_op jit(solution)/shard_map/ppermute | solution.py:290
  10.7 3.0 %collective-permute-start.17 = (bf16[96,640]{1,0:T(8,128)(2,1)S(1)}, bf16[96,640]{1,0:T(8,128)(2,1)S(1)}, u32[]{:S(2)}, u32[]{:S(2)}) collective-permute-start(bf16[96,640]{1,0:T(8,128)(2,1)S(1)} %constant_dynamic-slice_fusion), channel_id=1, source_target_pairs={{0,2},{1,3},{2,4},{3,5},{4,6},{5,7},{6,0},{7,1},{8,10},{9,11},{10,... | collective-permute-start | bytes 368648 | tf_op jit(solution)/shard_map/ppermute | solution.py:290
  13.7 2.1 collective-permute-start.16
  19.1 6.8 %shard_map.94 = (bf16[8,208,384]{2,1,0:T(8,128)(2,1)}, bf16[1536,384]{1,0:T(8,128)(2,1)S(1)}, bf16[128,128]{1,0:T(8,128)(2,1)}, s32[2]{0:T(128)}) custom-call(s32[2]{0:T(128)} %pad_add_fusion.place, s32[5,64]{1,0:T(8,128)} %bitcast.12, f32[8,128]{1,0:T(8,128)} %constant.28.clone.frequency, bf16[3,128,3072]{2,1,0:T(8,128)(2,1)} %rows_far.1, ...), custom_call_target="tpu_custom_call" | custom-call | flops 1000000000 | bytes 6000000 | tf_op jit(solution)/shard_map/pallas_call | solution.py:296
  26.7 39.0 %conditional.1 = (bf16[1536,384]{1,0:T(8,128)(2,1)}, bf16[8,208,384]{2,1,0:T(8,128)(2,1)}, bf16[192,640]{1,0:T(8,128)(2,1)}, bf16[96,640]{1,0:T(8,128)(2,1)}) conditional(s32[]{:T(128)} %clamp.3, (bf16[1536,384]{1,0:T(8,128)(2,1)S(1)}, bf16[8,208,384]{2,1,0:T(8,128)(2,1)}, bf16[192,640]{1,0:T(8,128)(2,1)S(1)}, ...), branch_computations={%region_1.0_spmd, %region_2.0_spmd, %region_3.0_spmd, %region_4.0_... | conditional | bytes 10027192 | solution.py:337
  26.7 5.2 %all-to-all-start = ((bf16[8,208,384]{2,1,0:T(8,128)(2,1)}), bf16[8,208,384]{2,1,0:T(8,128)(2,1)}, u32[]{:S(2)}, u32[]{:S(2)}) async-start(bf16[8,208,384]{2,1,0:T(8,128)(2,1)} %get-tuple-element.41), calls=%async_computation | async-start | bytes 2555904 | tf_op jit(solution)/shard_map/cond/branch_0_fun/all_to_all | solution.py:324
  31.9 2.1 collective-permute-start
  34.0 3.9 %collective-permute-start.1 = (bf16[192,640]{1,0:T(8,128)(2,1)S(1)}, bf16[192,640]{1,0:T(8,128)(2,1)}, u32[]{:S(2)}, u32[]{:S(2)}) collective-permute-start(bf16[192,640]{1,0:T(8,128)(2,1)S(1)} %get-tuple-element.42), channel_id=1, source_target_pairs={{0,6},{1,7},{2,0},{3,1},{4,2},{5,3},{6,4},{7,5},{8,14},{9,15},{10,... | collective-permute-start | bytes 737288 | tf_op jit(solution)/shard_map/cond/branch_0_fun/ppermute | solution.py:290
  38.1 24.2 %collective-permute-done.2 = bf16[96,640]{1,0:T(8,128)(2,1)} collective-permute-done((bf16[96,640]{1,0:T(8,128)(2,1)S(1)}, bf16[96,640]{1,0:T(8,128)(2,1)}, u32[]{:S(2)}, u32[]{:S(2)}) %collective-permute-start.2) | collective-permute-done | bytes 122912 | tf_op jit(solution)/shard_map/cond/branch_0_fun/ppermute | solution.py:290
  62.8 2.9 %all-to-all-done = bf16[8,208,384]{2,1,0:T(8,128)(2,1)} async-done(((bf16[8,208,384]{2,1,0:T(8,128)(2,1)}), bf16[8,208,384]{2,1,0:T(8,128)(2,1)}, u32[]{:S(2)}, u32[]{:S(2)}) %all-to-all-start) | async-done | bytes 1277984 | tf_op jit(solution)/shard_map/cond/branch_0_fun/all_to_all | solution.py:324
  68.6 10.8 %all-to-all-start.5 = ((bf16[8,192,384]{2,1,0:T(8,128)(2,1)}), bf16[8,192,384]{2,1,0:T(8,128)(2,1)S(1)}, u32[]{:S(2)}, u32[]{:S(2)}) async-start(bf16[8,192,384]{2,1,0:T(8,128)(2,1)} %bitcast.3), calls=%async_computation.5 | async-start | bytes 2359296 | tf_op jit(solution)/shard_map/all_to_all | solution.py:324
  79.3 3.8 %shard_map.95.first = bf16[512,384]{1,0:T(8,128)(2,1)} custom-call(s32[2]{0:T(128)} %get-tuple-element.88.info, bf16[8,208,384]{2,1,0:T(8,128)(2,1)} %get-tuple-element.99.blocks.extras), custom_call_target="tpu_custom_call" | custom-call | flops 1000000000 | bytes 2000000 | tf_op jit(solution)/shard_map/pallas_call | solution.py:350
  83.1 28.2 %all-to-all-done.5.blocks = bf16[8,192,384]{2,1,0:T(8,128)(2,1)S(1)} async-done(((bf16[8,192,384]{2,1,0:T(8,128)(2,1)}), bf16[8,192,384]{2,1,0:T(8,128)(2,1)S(1)}, u32[]{:S(2)}, u32[]{:S(2)}) %all-to-all-start.5) | async-done | bytes 1179680 | tf_op jit(solution)/shard_map/all_to_all | solution.py:324
  112.3 4.5 %shard_map.96 = (bf16[8,128,384]{2,1,0:T(8,128)(2,1)}, f32[32,384]{1,0:T(8,128)}) custom-call(s32[2]{0:T(128)} %get-tuple-element.88.info, bf16[512,384]{1,0:T(8,128)(2,1)} %shard_map.95.first, bf16[8,208,384]{2,1,0:T(8,128)(2,1)} %get-tuple-element.99.blocks.extras, bf16[8,192,384]{2,1,0:T(8,128)(2,1)} %copy-done.2), custom_call_target="tpu_custom_call" | custom-call | flops 1000000000 | bytes 4000000 | tf_op jit(solution)/shard_map/pallas_call | solution.py:358
  116.8 27.2 %all_to_all.45.back = bf16[8,128,384]{2,1,0:T(8,128)(2,1)} all-to-all(bf16[8,128,384]{2,1,0:T(8,128)(2,1)} %get-tuple-element.101), channel_id=1, replica_groups=mesh['dp'=32,'seq'=8] {'seq'}, dimensions={0} | all-to-all | bytes 1572864 | tf_op jit(solution)/shard_map/all_to_all | solution.py:324
  144.0 4.0 %shard_map.97 = (bf16[128,3072]{1,0:T(8,128)(2,1)}, bf16[32,128]{1,0:T(8,128)(2,1)}, bf16[32,48,128]{2,1,0:T(8,128)(2,1)}) custom-call(bf16[8,128,384]{2,1,0:T(8,128)(2,1)} %all_to_all.45.back, bf16[128,128]{1,0:T(8,128)(2,1)} %get-tuple-element.102.to_rows, bf16[32,3072]{1,0:T(8,128)(2,1)} %bitcast.11, bf16[128,5120]{1,0:T(8,128)(2,1)} %cotangent.1, ...), custom_call_target="tpu_custom_call" | custom-call | flops 100000000 | bytes 2000000 | tf_op jit(solution)/shard_map/pallas_call | solution.py:370
  148.0 21.8 %all_to_all.46.parts = bf16[32,48,128]{2,1,0:T(8,128)(2,1)} all-to-all(bf16[32,48,128]{2,1,0:T(8,128)(2,1)} %get-tuple-element.106), channel_id=1, replica_groups=mesh['dp'=32,'seq'=8] {'dp'}, dimensions={0} | all-to-all | bytes 786432 | tf_op jit(solution)/shard_map/all_to_all | solution.py:324
  171.5 3.4 %all-to-all-start.8 = ((f32[8,48,128]{2,1,0:T(8,128)}), f32[8,48,128]{2,1,0:T(8,128)S(1)}, u32[]{:S(2)}, u32[]{:S(2)}) async-start(f32[8,48,128]{2,1,0:T(8,128)} %shard_map.98), calls=%async_computation.8 | async-start | bytes 393216 | tf_op jit(solution)/shard_map/all_to_all | solution.py:324
  174.9 4.0 %shard_map.100.refs_4_ = bf16[128,5120]{1,0:T(8,128)(2,1)} custom-call(s32[1]{0:T(128)} %bitcast.shard, bf16[128,3072]{1,0:T(8,128)(2,1)} %get-tuple-element.104.attended, bf16[32,128]{1,0:T(8,128)(2,1)} %get-tuple-element.105.adapted, bf16[32,5120]{1,0:T(8,128)(2,1)} %up.5, bf16[3072,640]{1,0:T(8,128)(2,1)} %own.1), custom_call_target="tpu_custom_call" | custom-call | flops 503316480 | bytes 3932160 | tf_op jit(solution)/shard_map/pallas_call | solution.py:395
  178.9 4.4 %all-to-all-done.8.parts = f32[8,48,128]{2,1,0:T(8,128)S(1)} async-done(((f32[8,48,128]{2,1,0:T(8,128)}), f32[8,48,128]{2,1,0:T(8,128)S(1)}, u32[]{:S(2)}, u32[]{:S(2)}) %all-to-all-start.8) | async-done | bytes 196640 | tf_op jit(solution)/shard_map/all_to_all | solution.py:324
  183.9 1.8 shard_map.99
  185.7 7.3 %all-to-all-start.9 = ((bf16[32,64,128]{2,1,0:T(8,128)(2,1)}), bf16[32,64,128]{2,1,0:T(8,128)(2,1)S(1)}, u32[]{:S(2)}, u32[]{:S(2)}) async-start(bf16[32,64,128]{2,1,0:T(8,128)(2,1)} %shard_map.99), calls=%async_computation.9 | async-start | bytes 1048576 | tf_op jit(solution)/shard_map/all_to_all | solution.py:324
  193.0 13.5 %shard_map.101 = bf16[128,5120]{1,0:T(8,128)(2,1)} custom-call(s32[1]{0:T(128)} %bitcast.shard, bf16[128,3072]{1,0:T(8,128)(2,1)} %get-tuple-element.104.attended, bf16[32,128]{1,0:T(8,128)(2,1)} %get-tuple-element.105.adapted, bf16[32,5120]{1,0:T(8,128)(2,1)} %up.5, bf16[32,7,96,640]{3,2,1,0:T(8,128)(2,1)} %bitcast.7, ...), custom_call_target="tpu_custom_call", output_to_operand_aliasing={{}: (8, {})} | custom-call | flops 4026531840 | bytes 31457280 | tf_op jit(solution)/shard_map/pallas_call | solution.py:434
  207.3 2.5 %shard_map.102 = (f32[32,5120]{1,0:T(8,128)}, f32[32,3072]{1,0:T(8,128)}) custom-call(bf16[32,64,128]{2,1,0:T(8,128)(2,1)} %copy-done), custom_call_target="tpu_custom_call" | custom-call | tf_op jit(solution)/shard_map/pallas_call | solution.py:427
  (30 shorter events, 12.1 us)
Async XLA Ops:
  7.2 178.5 %all-gather.2.cloned.1.call-start = ((), (), s32[]{:S(2)}) async-start(), calls=%async_computation.10 | async-start | bytes 28385280 | tf_op jit(solution)/shard_map/all_gather | solution.py:347
  8.1 18.5 %collective-permute-start.18 = (bf16[96,640]{1,0:T(8,128)(2,1)S(1)}, bf16[96,640]{1,0:T(8,128)(2,1)S(1)}, u32[]{:S(2)}, u32[]{:S(2)}) collective-permute-start(bf16[96,640]{1,0:T(8,128)(2,1)S(1)} %constant_dynamic-slice_fusion), channel_id=1, source_target_pairs={{0,1},{1,2},{2,3},{3,4},{4,5},{5,6},{6,7},{7,0},{8,9},{9,10},{10,1... | collective-permute-start | bytes 368648 | tf_op jit(solution)/shard_map/ppermute | solution.py:290
  10.7 16.0 %collective-permute-start.17 = (bf16[96,640]{1,0:T(8,128)(2,1)S(1)}, bf16[96,640]{1,0:T(8,128)(2,1)S(1)}, u32[]{:S(2)}, u32[]{:S(2)}) collective-permute-start(bf16[96,640]{1,0:T(8,128)(2,1)S(1)} %constant_dynamic-slice_fusion), channel_id=1, source_target_pairs={{0,2},{1,3},{2,4},{3,5},{4,6},{5,7},{6,0},{7,1},{8,10},{9,11},{10,... | collective-permute-start | bytes 368648 | tf_op jit(solution)/shard_map/ppermute | solution.py:290
  13.7 12.9 %collective-permute-start.16 = (bf16[96,640]{1,0:T(8,128)(2,1)S(1)}, bf16[96,640]{1,0:T(8,128)(2,1)S(1)}, u32[]{:S(2)}, u32[]{:S(2)}) collective-permute-start(bf16[96,640]{1,0:T(8,128)(2,1)S(1)} %constant_dynamic-slice_fusion), channel_id=1, source_target_pairs={{0,6},{1,7},{2,0},{3,1},{4,2},{5,3},{6,4},{7,5},{8,14},{9,15},{10,... | collective-permute-start | bytes 368648 | tf_op jit(solution)/shard_map/ppermute | solution.py:290
  15.8 10.8 %collective-permute-start.15 = (bf16[96,640]{1,0:T(8,128)(2,1)S(1)}, bf16[96,640]{1,0:T(8,128)(2,1)S(1)}, u32[]{:S(2)}, u32[]{:S(2)}) collective-permute-start(bf16[96,640]{1,0:T(8,128)(2,1)S(1)} %constant_dynamic-slice_fusion), channel_id=1, source_target_pairs={{0,7},{1,0},{2,1},{3,2},{4,3},{5,4},{6,5},{7,6},{8,15},{9,8},{10,9... | collective-permute-start | bytes 368648 | tf_op jit(solution)/shard_map/ppermute | solution.py:290
  26.7 39.0 %all-to-all-start = ((bf16[8,208,384]{2,1,0:T(8,128)(2,1)}), bf16[8,208,384]{2,1,0:T(8,128)(2,1)}, u32[]{:S(2)}, u32[]{:S(2)}) async-start(bf16[8,208,384]{2,1,0:T(8,128)(2,1)} %get-tuple-element.41), calls=%async_computation | async-start | bytes 2555904 | tf_op jit(solution)/shard_map/cond/branch_0_fun/all_to_all | solution.py:324
  31.9 30.9 %collective-permute-start = (bf16[1536,384]{1,0:T(8,128)(2,1)S(1)}, bf16[1536,384]{1,0:T(8,128)(2,1)}, u32[]{:S(2)}, u32[]{:S(2)}) collective-permute-start(bf16[1536,384]{1,0:T(8,128)(2,1)S(1)} %get-tuple-element.40), channel_id=1, source_target_pairs={{0,8},{8,0},{16,24},{24,16},{32,40},{40,32},{48,56},{56,48},{64,72... | collective-permute-start | bytes 3538952 | tf_op jit(solution)/shard_map/cond/branch_0_fun/ppermute | solution.py:331
  34.0 28.8 %collective-permute-start.1 = (bf16[192,640]{1,0:T(8,128)(2,1)S(1)}, bf16[192,640]{1,0:T(8,128)(2,1)}, u32[]{:S(2)}, u32[]{:S(2)}) collective-permute-start(bf16[192,640]{1,0:T(8,128)(2,1)S(1)} %get-tuple-element.42), channel_id=1, source_target_pairs={{0,6},{1,7},{2,0},{3,1},{4,2},{5,3},{6,4},{7,5},{8,14},{9,15},{10,... | collective-permute-start | bytes 737288 | tf_op jit(solution)/shard_map/cond/branch_0_fun/ppermute | solution.py:290
  37.9 24.5 %collective-permute-start.2 = (bf16[96,640]{1,0:T(8,128)(2,1)S(1)}, bf16[96,640]{1,0:T(8,128)(2,1)}, u32[]{:S(2)}, u32[]{:S(2)}) collective-permute-start(bf16[96,640]{1,0:T(8,128)(2,1)S(1)} %get-tuple-element.43), channel_id=1, source_target_pairs={{0,1},{1,2},{2,3},{3,4},{4,5},{5,6},{6,7},{7,0},{8,9},{9,10},{10,1... | collective-permute-start | bytes 368648 | tf_op jit(solution)/shard_map/cond/branch_0_fun/ppermute | solution.py:290
  67.6 0.9 copy-start.1
  68.6 42.7 %all-to-all-start.5 = ((bf16[8,192,384]{2,1,0:T(8,128)(2,1)}), bf16[8,192,384]{2,1,0:T(8,128)(2,1)S(1)}, u32[]{:S(2)}, u32[]{:S(2)}) async-start(bf16[8,192,384]{2,1,0:T(8,128)(2,1)} %bitcast.3), calls=%async_computation.5 | async-start | bytes 2359296 | tf_op jit(solution)/shard_map/all_to_all | solution.py:324
  111.3 1.0 copy-start.2
  171.5 11.7 %all-to-all-start.8 = ((f32[8,48,128]{2,1,0:T(8,128)}), f32[8,48,128]{2,1,0:T(8,128)S(1)}, u32[]{:S(2)}, u32[]{:S(2)}) async-start(f32[8,48,128]{2,1,0:T(8,128)} %shard_map.98), calls=%async_computation.8 | async-start | bytes 393216 | tf_op jit(solution)/shard_map/all_to_all | solution.py:324
  183.2 0.7 copy-start.3
  185.7 20.8 %all-to-all-start.9 = ((bf16[32,64,128]{2,1,0:T(8,128)(2,1)}), bf16[32,64,128]{2,1,0:T(8,128)(2,1)S(1)}, u32[]{:S(2)}, u32[]{:S(2)}) async-start(bf16[32,64,128]{2,1,0:T(8,128)(2,1)} %shard_map.99), calls=%async_computation.9 | async-start | bytes 1048576 | tf_op jit(solution)/shard_map/all_to_all | solution.py:324
  206.5 0.8 copy-start
Sparse Core Ops, SparseCore 0:
  68.7 114.9 all-gather.1
